TPU v7x, 32 devices: a whole 2x2x4 slice. The times are simulated.
32 devices in a mesh: dp: 8 (over z, y), mp: 4 (over x, core).
Axes of the slice: x: 2, y: 2, z: 4, core: 2. Of those that a mesh axis runs over, the one named last changes fastest.
Arguments:
- tokens: bfloat16 [16384, 768], P('dp'), may hold values from -6 to 6
- cotangent: bfloat16 [16384, 768], P('dp'), may hold values from -6 to 6
- seq_lengths: int32 [32], replicated, may hold values from 1 to 768, as said below
- seq_bin: int32 [32], replicated, may hold values from 0 to 15, as said below
- qkv_weight: bfloat16 [3, 768, 768], P(None, 'dp', 'mp'), may hold values from -0.21875 to 0.21875
- out_weight: bfloat16 [768, 768], P('mp', 'dp'), may hold values from -0.875 to 0.875
- up_weight: bfloat16 [768, 3072], P('dp', 'mp'), may hold values from -0.21875 to 0.21875
- down_weight: bfloat16 [3072, 768], P('mp', 'dp'), may hold values from -0.109375 to 0.109375
- norm_gains: float32 [2, 768], replicated, may hold values from 0.5 to 1.5
- shared_biases: float32 [4, 768], replicated, may hold values from -1.8 to 1.8
- head_biases: float32 [2, 768], P(None, 'mp'), may hold values from -1.8 to 1.8
- unit_bias: float32 [3072], P('mp'), may hold values from -0.6 to 0.6
- qkv_moment: float32 [3, 768, 768], P(None, 'dp', 'mp'), may hold values from -768 to 768
- out_moment: float32 [768, 768], P('mp', 'dp'), may hold values from -192 to 192
- up_moment: float32 [768, 3072], P('dp', 'mp'), may hold values from -128 to 128
- down_moment: float32 [3072, 768], P('mp', 'dp'), may hold values from -320 to 320
- gain_moment: float32 [2, 768], replicated, may hold values from -640 to 640
- bias_moment: float32 [4, 768], replicated, may hold values from -640 to 640
- head_moment: float32 [2, 768], P(None, 'mp'), may hold values from -640 to 640
- unit_moment: float32 [3072], P('mp'), may hold values from -128 to 128
Outputs:
- block_out: float32 [16384, 768], P('dp')
- input_grad: float32 [16384, 768], P('dp')
- qkv_moment_next: float32 [3, 768, 768], P(None, 'dp', 'mp')
- qkv_next: float32 [3, 768, 768], P(None, 'dp', 'mp')
- out_moment_next: float32 [768, 768], P('mp', 'dp')
- out_next: float32 [768, 768], P('mp', 'dp')
- up_moment_next: float32 [768, 3072], P('dp', 'mp')
- up_next: float32 [768, 3072], P('dp', 'mp')
- down_moment_next: float32 [3072, 768], P('mp', 'dp')
- down_next: float32 [3072, 768], P('mp', 'dp')
- gain_moment_next: float32 [2, 768], replicated
- gain_next: float32 [2, 768], replicated
- bias_moment_next: float32 [4, 768], replicated
- bias_next: float32 [4, 768], replicated
- head_moment_next: float32 [2, 768], P(None, 'mp')
- head_next: float32 [2, 768], P(None, 'mp')
- unit_moment_next: float32 [3072], P('mp')
- unit_next: float32 [3072], P('mp')
Inputs may be any that keep to these rules, and one draw needn't show every extreme that they name: `seq_lengths`: one sequence is exactly 768 long. Sequence s lies in bin seq_bin[s]; bin b (rows b * 1024 to (b + 1) * 1024 - 1 of tokens, on index b // 2 of dp) holds exactly two sequences, packed from its first row in the order of their indices; their lengths add up to 1024 or less, and the rows after them are unused.
All inputs are finite; a program needn't handle non-finite values.
Results may differ from a plain program's by a relative error of at most 0.024.
Values may be sent and summed in bfloat16 or wider, within the bound.
No kernel may reach another device: no remote copies, remote signals or barrier semaphores. Data moves between devices by JAX's collectives and lax.ppermute only.
A program may use at most 192 MiB of HBM per device.

v0:
```python
import math

import jax
import jax.numpy as jnp
from jax import lax
from jax.experimental import pallas as pl
from jax.experimental.pallas import tpu as pltpu
from jax.sharding import Mesh, PartitionSpec as P

D = 768
HEAD_DIM = 64
FF = 3072
SLOTS = 1024
NS_STEPS = 5

EPS = 1e-05
MOMENTUM = 0.9
NS_A = 3.4445
NS_B = -4.775
NS_C = 2.0315
RATE = 1.0
DECAY = 0.01
VECTOR_RATE = 0.1
FLOOR = -1e30
TILE = 256
SHIFTS = (0.0, 0.0, 0.3, 0.8, 0.8)
ROWS = 256

BF = jnp.bfloat16
F32 = jnp.float32


def swap(value, axis, distance=1):
    size = lax.axis_size(axis)
    return lax.ppermute(value, axis, [(i, i ^ distance) for i in range(size)])


def join(mine, theirs, bit, dim):
    low = jnp.where(bit, theirs, mine)
    high = jnp.where(bit, mine, theirs)
    return jnp.stack((low, high), axis=dim)


def distances(axis):
    found = []
    step = lax.axis_size(axis) // 2
    while step >= 1:
        found.append(step)
        step //= 2
    return found


def bit_of(axis, distance=1):
    return (lax.axis_index(axis) // distance) % 2 == 1


def after(value, *others):
    return lax.optimization_barrier((value, *others))[0]


def fixed(value):
    return lax.optimization_barrier(value.astype(BF))


def fixed32(value):
    return lax.optimization_barrier(value)


def grow(piece, axis, distance, dim, *wait):
    got = swap(piece, axis, distance)
    if wait:
        got = after(got, *wait)
    return join(piece, got, bit_of(axis, distance), dim)


def take(value, bit, dim):
    low, high = (lax.index_in_dim(value, k, dim, keepdims=False) for k in (0, 1))
    keep = jnp.where(bit, high, low)
    send = jnp.where(bit, low, high)
    return keep, send


def offer(value, axis, dim, distance):
    keep, send = take(value, bit_of(axis, distance), dim)
    send = fixed(send)
    return keep, send, swap(send, axis, distance)


def settle(offered, *wait):
    keep, _, got = offered
    if wait:
        got = after(got, *wait)
    return keep.astype(F32) + got.astype(F32)


def split_planes(value, dim):
    bits = [2 for _ in distances("z")]
    return value.reshape(*value.shape[:dim], *bits, *value.shape[dim + 1 :])


def by_rows(grad):
    return grad.reshape(lax.axis_size("z"), 2, -1, grad.shape[-1])


def all_sum(value, axes):
    for axis in axes:
        for distance in distances(axis):
            value = value + swap(value, axis, distance)
    return value


def swap_cores(own):
    half = own.shape[0] // 2
    return jnp.concatenate((swap(own[:half], "c"), swap(own[half:], "c")), axis=0)


def across_cores(partial_value):
    own = fixed(partial_value)
    return own.astype(F32) + swap_cores(own).astype(F32)


def layer_norm(rows, gain, shift):
    centre = rows - jnp.mean(rows, axis=-1, keepdims=True)
    spread = jnp.mean(centre * centre, axis=-1, keepdims=True)
    return centre * lax.rsqrt(spread + EPS) * gain + shift


def segments_of(seq_lengths, seq_bin, index):
    count = seq_lengths.shape[0]
    order = jnp.arange(count, dtype=jnp.int32)
    inside = seq_bin == index
    leader = jnp.min(jnp.where(inside, order, count))
    first = jnp.sum(jnp.where(order == leader, seq_lengths, 0))
    total = jnp.sum(jnp.where(inside, seq_lengths, 0))
    slot = jnp.arange(SLOTS, dtype=jnp.int32)
    segment = jnp.where(slot < first, 0, jnp.where(slot < total, 1, slot + 2))
    return (segment, slot < total)


def first_key(seq_lengths, seq_bin, index):
    segment, valid = segments_of(seq_lengths, seq_bin, index)
    slot = jnp.arange(SLOTS, dtype=jnp.int32)
    start = jnp.sum(jnp.where(segment == 0, 1, 0))
    low = jnp.where(segment == 0, 0, jnp.where(segment == 1, start, slot))
    return low, valid


def dot_nt(left, right):
    return lax.dot_general(left, right, (((1,), (1,)), ((), ())), preferred_element_type=F32)


def dot_tn(left, right):
    return lax.dot_general(left, right, (((0,), (0,)), ((), ())), preferred_element_type=F32)


def tile_mask(low, tile, keys):
    shape = (TILE, keys)
    row = lax.broadcasted_iota(jnp.int32, shape, 0) + tile * TILE
    column = lax.broadcasted_iota(jnp.int32, shape, 1)
    return (column <= row) & (column >= low)


def attend_kernel(low_ref, qkv_ref, out_ref, log_ref):
    width = out_ref.shape[1]
    for tile in range(SLOTS // TILE):
        here = slice(tile * TILE, (tile + 1) * TILE)
        keys = (tile + 1) * TILE
        mask = tile_mask(low_ref[here], tile, keys)
        for head in range(width // HEAD_DIM):
            lanes = slice(head * HEAD_DIM, (head + 1) * HEAD_DIM)
            query = qkv_ref[here, lanes]
            key = qkv_ref[:keys, width + head * HEAD_DIM : width + (head + 1) * HEAD_DIM]
            value = qkv_ref[:keys, 2 * width + head * HEAD_DIM : 2 * width + (head + 1) * HEAD_DIM]
            scores = jnp.where(mask, dot_nt(query, key), FLOOR)
            top = jnp.max(scores, axis=-1, keepdims=True)
            raised = jnp.exp(scores - top)
            total = jnp.sum(raised, axis=-1, keepdims=True)
            weights = (raised * (1.0 / total)).astype(BF)
            mixed = jnp.dot(weights, value, preferred_element_type=F32)
            out_ref[here, lanes] = mixed.astype(BF)
            log_ref[here, lanes] = jnp.broadcast_to(top + jnp.log(total), (TILE, HEAD_DIM))


def attend_back_kernel(low_ref, qkv_ref, grad_ref, log_ref, out_ref, keys_sum, values_sum):
    width = grad_ref.shape[1]
    for head in range(width // HEAD_DIM):
        lanes = slice(head * HEAD_DIM, (head + 1) * HEAD_DIM)
        key_lanes = slice(width + head * HEAD_DIM, width + (head + 1) * HEAD_DIM)
        value_lanes = slice(2 * width + head * HEAD_DIM, 2 * width + (head + 1) * HEAD_DIM)
        keys_sum[...] = jnp.zeros_like(keys_sum)
        values_sum[...] = jnp.zeros_like(values_sum)
        for tile in range(SLOTS // TILE):
            here = slice(tile * TILE, (tile + 1) * TILE)
            keys = (tile + 1) * TILE
            mask = tile_mask(low_ref[here], tile, keys)
            query = qkv_ref[here, lanes]
            key = qkv_ref[:keys, key_lanes]
            value = qkv_ref[:keys, value_lanes]
            grad = grad_ref[here, lanes]
            scores = dot_nt(query, key) - log_ref[here, head * HEAD_DIM : head * HEAD_DIM + 1]
            weights = jnp.exp(jnp.where(mask, scores, FLOOR))
            grad_weights = dot_nt(grad, value)
            product = weights * grad_weights
            inner = jnp.sum(product, axis=-1, keepdims=True)
            grad_scores = (product - weights * inner).astype(BF)
            values_sum[:keys] += dot_tn(weights.astype(BF), grad)
            keys_sum[:keys] += dot_tn(grad_scores, query)
            grad_query = jnp.dot(grad_scores, key, preferred_element_type=F32).astype(BF)
            out_ref[here, lanes] = (grad_query.astype(F32) * HEAD_DIM ** (-0.5)).astype(BF)
        out_ref[:, key_lanes] = keys_sum[...].astype(BF)
        out_ref[:, value_lanes] = values_sum[...].astype(BF)


def on_chip(kernel, shapes, scratch, flops, exps, *operands):
    moved = sum(o.size * o.dtype.itemsize for o in (*operands, *shapes))
    return pl.pallas_call(
        kernel,
        out_shape=shapes,
        in_specs=[pl.BlockSpec(memory_space=pltpu.VMEM)] * len(operands),
        out_specs=[pl.BlockSpec(memory_space=pltpu.VMEM)] * len(shapes),
        scratch_shapes=scratch,
        compiler_params=pltpu.CompilerParams(vmem_limit_bytes=50 * 2**20),
        cost_estimate=pl.CostEstimate(flops=flops, bytes_accessed=moved, transcendentals=exps),
    )(*operands)


def attend(low, qkv):
    width = qkv.shape[1] // 3
    shapes = [
        jax.ShapeDtypeStruct((SLOTS, width), BF),
        jax.ShapeDtypeStruct((SLOTS, width), F32),
    ]
    pairs = SLOTS * SLOTS * width // HEAD_DIM
    return on_chip(attend_kernel, shapes, [], 16 * pairs * HEAD_DIM, pairs, low, qkv)


def attend_back(low, qkv, grad, log_total):
    shapes = [jax.ShapeDtypeStruct(qkv.shape, BF)]
    scratch = [pltpu.VMEM((SLOTS, HEAD_DIM), F32)] * 2
    pairs = SLOTS * SLOTS * grad.shape[1] // HEAD_DIM
    return on_chip(
        attend_back_kernel, shapes, scratch, 40 * pairs * HEAD_DIM, pairs, low, qkv, grad, log_total
    )[0]


def newton_kernel(
    wide_ref, factor_ref, terms_ref, gram_ref, panel_ref, out_ref, rest, rh, poly, ph, pl_, total, th
):
    factor = factor_ref[0]
    spans = [slice(k * ROWS, (k + 1) * ROWS) for k in range(D // ROWS)]

    def diagonal(span):
        row = lax.broadcasted_iota(jnp.int32, (ROWS, D), 0) + span.start
        column = lax.broadcasted_iota(jnp.int32, (ROWS, D), 1)
        return row == column

    def parts(value):
        high = value.astype(BF)
        return high, (value - high.astype(F32)).astype(BF)

    def times_poly(value, fine):
        high, low = parts(value)
        result = jnp.dot(high, ph[...], preferred_element_type=F32)
        if fine:
            result += jnp.dot(high, pl_[...], preferred_element_type=F32)
            result += jnp.dot(low, ph[...], preferred_element_type=F32)
        return result

    def make_poly(line):
        for span in spans:
            square = jnp.dot(rh[span], rh[...], preferred_element_type=F32)
            value = line * rest[span] + NS_C * square
            poly[span] = value
            ph[span], pl_[span] = parts(value)

    def terms(step):
        return [terms_ref[4 * step + k] for k in range(4)]

    def wide_step(step, fine, last):
        shift, unit, line, shift_next = terms(step)
        make_poly(line)
        for span in spans:
            value = unit * total[span] + times_poly(total[span], False)
            total[span] = value
            if last:
                th[span] = value.astype(BF)
        if not last:
            for span in spans:
                value = unit * rest[span] + times_poly(rest[span], fine) + shift * poly[span]
                value = jnp.where(diagonal(span), value + unit * shift, value)
                value = unit * value + times_poly(value, fine)
                value = jnp.where(diagonal(span), value - shift_next, value)
                rest[span] = value
                rh[span] = value.astype(BF)

    @pl.when(wide_ref[0] == 1)
    def _():
        for span in spans:
            value = gram_ref[span] * (factor * factor)
            rest[span] = value
            rh[span] = value.astype(BF)
            total[span] = jnp.where(diagonal(span), 1.0, 0.0)

        @pl.loop(0, 2)
        def _(step):
            wide_step(step, True, False)

        @pl.loop(2, NS_STEPS - 1)
        def _(step):
            wide_step(step, False, False)

        wide_step(NS_STEPS - 1, False, True)
        for span in spans:
            value = jnp.dot(th[span], panel_ref[...], preferred_element_type=F32)
            out_ref[span] = (value * factor).astype(BF)

    @pl.when(wide_ref[0] == 0)
    def _():
        for span in spans:
            value = panel_ref[span].astype(F32) * factor
            total[span] = value
            th[span] = value.astype(BF)

        @pl.loop(0, NS_STEPS)
        def _(step):
            shift, unit, line, _ = terms(step)
            for span in spans:
                value = dot_nt(th[span], th[...])
                value = jnp.where(diagonal(span), value - shift, value)
                rest[span] = value
                rh[span] = value.astype(BF)
            make_poly(line)
            for span in spans:
                value = jnp.dot(ph[...], th[:, span], preferred_element_type=F32)
                value = unit * total[:, span] + value
                total[:, span] = value
                th[:, span] = value.astype(BF)

        for span in spans:
            out_ref[span] = th[span]


def newton(is_wide, factor, gram, panel):
    shape = jax.ShapeDtypeStruct(panel.shape, BF)
    whole, scalar = (pl.BlockSpec(memory_space=m) for m in (pltpu.VMEM, pltpu.SMEM))
    terms = []
    for step, shift in enumerate(SHIFTS):
        unit = NS_A + NS_B * shift + NS_C * shift * shift
        following = SHIFTS[step + 1] if step + 1 < NS_STEPS else 0.0
        terms += [shift, unit, NS_B + 2 * NS_C * shift, following]
    full, half = pltpu.VMEM((D, D), F32), pltpu.VMEM((D, D), BF)
    return pl.pallas_call(
        newton_kernel,
        out_shape=shape,
        in_specs=[scalar, scalar, scalar, whole, whole],
        out_specs=whole,
        scratch_shapes=[full, half, full, half, half, full, half],
        compiler_params=pltpu.CompilerParams(vmem_limit_bytes=50 * 2**20),
        cost_estimate=pl.CostEstimate(
            flops=25 * 2 * D**3, bytes_accessed=5 * 2**20, transcendentals=0
        ),
    )(is_wide.astype(jnp.int32)[None], factor[None], jnp.array(terms, F32), gram, panel)


def on_device(
    tokens,
    cotangent,
    seq_lengths,
    seq_bin,
    qkv_weight,
    out_weight,
    up_weight,
    down_weight,
    norm_gains,
    shared_biases,
    head_biases,
    unit_bias,
    qkv_moment,
    out_moment,
    up_moment,
    down_moment,
    gain_moment,
    bias_moment,
    head_moment,
    unit_moment,
):
    x_index = lax.axis_index("x")
    groups = lax.axis_size("z") * lax.axis_size("y")
    position = lax.axis_index("z") * lax.axis_size("y") + lax.axis_index("y")
    rows_each = qkv_weight.shape[1]
    heads_each = qkv_weight.shape[2]
    units_each = up_weight.shape[1]
    scale = HEAD_DIM ** (-0.5)

    z_steps = distances("z")
    qkv_piece = jnp.concatenate([qkv_weight[t] for t in range(3)], axis=1)
    qkv_piece = grow(qkv_piece, "z", z_steps[0], 0)
    early = qkv_piece
    for lead, distance in enumerate(z_steps[1:]):
        qkv_piece = grow(qkv_piece, "z", distance, lead + 1)
    depth = len(z_steps)
    up_weight_now, out_weight_now, down_weight_now = lax.optimization_barrier(
        (up_weight, out_weight, down_weight, early)
    )[:3]
    up_piece = jnp.concatenate((up_weight_now, out_weight_now.T), axis=1)
    down_piece = fixed(down_weight_now.T)
    down_piece = jnp.stack((down_piece, after(swap(down_piece, "x"), qkv_piece)))
    up_piece = grow(up_piece, "z", z_steps[0], 0, qkv_piece)
    qkv_own = grow(qkv_piece, "y", 1, depth, up_piece, down_piece)
    qkv_own = qkv_own.reshape(-1, qkv_own.shape[-1])
    qkv = [qkv_own, swap(qkv_own, "x")]

    biases = after(jnp.concatenate((head_biases.reshape(-1), unit_bias)), early)
    small = (biases, swap(biases, "x"))
    zero = jnp.zeros((heads_each,), F32)
    scales = jnp.concatenate((jnp.full((heads_each,), scale, F32), jnp.ones((2 * heads_each,), F32)))

    def project(group):
        shift = jnp.concatenate(
            (small[group][:heads_each], zero, small[group][heads_each : 2 * heads_each])
        )
        value = jnp.dot(normed, qkv[group], preferred_element_type=F32)
        return ((value + shift) * scales).astype(BF)

    start = x_index * SLOTS
    tokens_now, lengths_now = lax.optimization_barrier((tokens, seq_lengths, early))[:2]
    rows = lax.dynamic_slice_in_dim(tokens_now, start, SLOTS, axis=0)
    low, valid = first_key(lengths_now, seq_bin, position * 2 + x_index)
    low = low[:, None]
    source = rows.astype(F32)
    normed = layer_norm(source, norm_gains[0], shared_biases[0]).astype(BF)
    heads = [project(0)]
    for lead, distance in enumerate(z_steps[1:]):
        up_piece = grow(up_piece, "z", distance, lead + 1, heads[0])
    down_piece = grow(down_piece, "z", z_steps[0], 1, up_piece)
    mixed, logs = attend(low, after(heads[0], down_piece))
    up_own = grow(up_piece, "y", 1, depth, mixed).reshape(-1, up_piece.shape[-1])
    out_own, up_own = up_own[:, units_each:], up_own[:, :units_each]
    out = (out_own, swap(out_own, "x"))
    up_own = fixed(up_own)
    up = (up_own, swap(up_own, "x"))
    for lead, distance in enumerate(z_steps[1:]):
        down_piece = grow(down_piece, "z", distance, lead + 2, up_own)
    qkv[1] = after(qkv[1], down_piece, up_own)
    heads.append(project(1))
    mixed_x, logs_x = attend(low, heads[1])
    mixed, logs = (mixed, mixed_x), (logs, logs_x)
    down_full = grow(down_piece, "y", 1, depth + 1, mixed_x)
    down_full = down_full.reshape(2, -1, down_piece.shape[-1])
    down = (down_full[0], down_full[1])
    branch = across_cores(dot_nt(mixed[0], out[0]) + dot_nt(mixed[1], out[1]))
    branch = after(branch, up[1], down_full)
    hidden = source + (branch + shared_biases[2])
    normed_two = layer_norm(hidden, norm_gains[1], shared_biases[1]).astype(BF)
    before = [
        jnp.dot(normed_two, up[k], preferred_element_type=F32) + small[k][2 * heads_each :]
        for k in range(2)
    ]
    active = [jax.nn.gelu(b).astype(BF) for b in before]

    grad_rows = lax.dynamic_slice_in_dim(cotangent, start, SLOTS, axis=0)
    grad_rows = grad_rows * valid[:, None].astype(BF)
    grad_result = grad_rows.astype(F32)
    grad_before = [
        jax.vjp(jax.nn.gelu, before[k])[1](
            jnp.dot(grad_rows, down[k], preferred_element_type=F32)
        )[0].astype(BF)
        for k in range(2)
    ]
    grad_partial = fixed(dot_nt(grad_before[0], up[0]) + dot_nt(grad_before[1], up[1]))
    grad_other = swap_cores(grad_partial)
    planes = lax.axis_size("z")
    held, held_two = after(tuple(active), grad_partial), after(normed_two, grad_partial)
    grad_down = jnp.stack([by_rows(dot_tn(grad_rows, held[k]).astype(BF)) for k in range(2)])
    down_offer = offer(grad_down, "y", 2, 1)
    grad_up = [
        dot_tn(after(held_two, down_offer[1]), grad_before[k]).astype(BF) for k in range(2)
    ]
    partial_two = fixed(dot_nt(active[0], down[0]) + dot_nt(active[1], down[1]))

    grad_normed_two = grad_partial.astype(F32) + grad_other.astype(F32)
    grad_hidden, grad_gain_two, grad_shift_two = jax.vjp(
        layer_norm, hidden, norm_gains[1], shared_biases[1]
    )[1](grad_normed_two)
    grad_hidden = grad_hidden + grad_result
    grad_branch = grad_hidden.astype(BF)
    grad_mixed = [jnp.dot(grad_branch, out[k], preferred_element_type=F32).astype(BF) for k in range(2)]
    grad_out = [dot_tn(grad_branch, mixed[k]).astype(BF) for k in range(2)]
    grad_up = [jnp.concatenate(pair, axis=1) for pair in zip(grad_up, grad_out)]
    grad_up_x = fixed(grad_up[1])
    up_got = swap(grad_up_x, "x")
    back_x = attend_back(low, heads[1], after(grad_mixed[1], grad_up_x, down_offer[1]), logs[1])
    grad_square_x = fixed(dot_tn(normed, back_x))
    square_got = swap(grad_square_x, "x")
    down_sum = split_planes(settle(down_offer, grad_square_x), 1)
    down_offer = offer(down_sum, "z", depth, z_steps[-1])
    up_sum = grad_up[0].astype(F32) + after(up_got, down_offer[1]).astype(F32)
    up_offer = offer(by_rows(up_sum), "y", 1, 1)
    grad_mixed[0] = after(grad_mixed[0], up_offer[1], down_offer[1])
    back = attend_back(low, heads[0], grad_mixed[0], logs[0])
    grad_square = dot_tn(normed, back).astype(BF)

    def next_down(lead, offered, last):
        summed = settle(offered, last)
        return offer(summed, "z", lead, z_steps[lead - 1])

    for lead in range(depth - 1, 0, -1):
        down_offer = next_down(lead, down_offer, grad_square)
    up_sum = split_planes(settle(up_offer, down_offer[1]), 0)
    up_offer = offer(up_sum, "z", depth - 1, z_steps[-1])
    square = grad_square.astype(F32) + after(square_got, up_offer[1]).astype(F32)
    square_offer = offer(by_rows(square), "y", 1, 1)
    down_sum = settle(down_offer, square_offer[1])
    down_sent = fixed(down_sum[1])
    down_got = swap(down_sent, "x")
    last = down_sent
    for lead in range(depth - 1, 0, -1):
        up_offer = offer(settle(up_offer, last), "z", lead - 1, z_steps[lead - 1])
        last = up_offer[1]
    square = split_planes(settle(square_offer, last), 0)
    square_offer = offer(square, "z", depth - 1, z_steps[-1])
    sum_down = down_sum[0] + after(down_got, square_offer[1]).astype(F32)
    sum_up = settle(up_offer, sum_down)
    sum_out, sum_up = sum_up[:, units_each:], sum_up[:, :units_each]

    grad_partial = fixed(dot_nt(back, qkv[0]) + dot_nt(back_x, qkv[1]))
    grad_normed = grad_partial.astype(F32) + swap_cores(grad_partial).astype(F32)
    grad_source, grad_gain_one, grad_shift_one = jax.vjp(
        layer_norm, source, norm_gains[0], shared_biases[0]
    )[1](grad_normed)
    result = hidden + (
        (partial_two.astype(F32) + swap_cores(partial_two).astype(F32)) + shared_biases[3]
    )
    def by_x(mine, theirs):
        return join(mine, theirs, bit_of("x"), 1)

    grad_bias = [jnp.sum(b.astype(F32), axis=0) for b in (back, back_x)]
    grad_heads = [jnp.stack((g[:heads_each], g[2 * heads_each :])) for g in grad_bias]
    grad_units = [jnp.sum(g.astype(F32), axis=0)[None] for g in grad_before]
    vectors = (
        jnp.stack((grad_gain_one, grad_gain_two)),
        jnp.stack(
            (
                grad_shift_one,
                grad_shift_two,
                jnp.sum(grad_branch.astype(F32), axis=0),
                jnp.sum(grad_result, axis=0),
            )
        ),
        by_x(*grad_heads),
        by_x(*grad_units),
    )
    sizes = [v.size for v in vectors]
    flat = jnp.concatenate([v.reshape(-1) for v in vectors]).reshape(-1, 128)
    moments = (
        qkv_moment[0],
        qkv_moment[1],
        qkv_moment[2],
        out_moment.T,
        up_moment,
        down_moment.T,
    )
    spread = groups // 8
    owners = [number * spread for number in (0, 3, 4, 7, 2, 5)]

    def to_owners(numbers, grads):
        nexts = [MOMENTUM * moments[k] + grad for k, grad in zip(numbers, grads)]
        panels = [(grad + MOMENTUM * m).astype(BF) for m, grad in zip(nexts, grads)]
        width = panels[0].shape[1]
        outgoing = jnp.zeros((groups, rows_each, width), BF)
        for number, panel in zip(numbers, panels):
            outgoing = outgoing.at[owners[number]].set(panel)
        incoming = lax.all_to_all(outgoing, ("z", "y"), split_axis=0, concat_axis=0, tiled=True)
        return nexts, incoming.reshape(groups * rows_each, width)

    def swap_parts(value, axis):
        half = value.shape[0] // 2
        return jnp.concatenate((swap(value[:half], axis), swap(value[half:], axis)), axis=0)

    wide_nexts, wide = to_owners((4, 5), (sum_up, sum_down))
    last = wide
    for lead in range(depth - 1, 0, -1):
        square_offer = offer(settle(square_offer, wide_nexts[1]), "z", lead - 1, z_steps[lead - 1])
        wide = after(wide, square_offer[1])
    gram = dot_nt(wide, wide).reshape(2, D // 2, D)
    keep, send = take(gram, bit_of("c"), 0)
    send = fixed32(send)
    gram_sent = swap_parts(send, "c")
    sum_square = settle(square_offer, send)
    narrow_grads = [sum_square[:, k * heads_each : (k + 1) * heads_each] for k in range(3)]
    narrow_nexts, narrow = to_owners((0, 1, 2, 3), (*narrow_grads, sum_out))
    gram = fixed32(keep + after(gram_sent, sum_square))
    gram_got = swap_parts(gram, "x")
    narrow = after(narrow, gram)
    pair = jnp.concatenate((narrow, swap(narrow, "x")), axis=1)
    flat = flat + after(swap(flat, "x"), narrow)
    pair = jnp.concatenate((pair, swap(pair, "c")), axis=1)
    flat = flat + after(swap(flat, "y"), pair)
    gram = gram + after(gram_got, pair, flat)
    half = SLOTS // 2
    core = lax.axis_index("c")
    finals = [fixed(after(result, gram)), fixed(after(grad_hidden + grad_source, gram))]
    got = [swap(lax.dynamic_slice_in_dim(v, core * half, half, axis=0), "x") for v in finals]
    gram = join(gram, swap_parts(gram, "c"), bit_of("c"), 0).reshape(D, D)
    is_wide = (position == owners[4]) | (position == owners[5])
    pair_values = pair.astype(F32)
    norm = jnp.where(is_wide, jnp.trace(gram), jnp.sum(pair_values * pair_values))
    factor = 1.0 / (jnp.sqrt(norm) + 1e-07)
    orth = newton(is_wide, factor, gram, jnp.where(is_wide, wide, pair))
    got, flat, back_sent = lax.optimization_barrier((got, flat, orth))
    back = lax.all_to_all(
        back_sent.reshape(groups, rows_each, units_each),
        ("z", "y"),
        split_axis=0,
        concat_axis=0,
        tiled=True,
    ).astype(F32)
    flat = all_sum(flat, ("z",)).reshape(-1)

    def both_bins(own, received):
        other = join(received, swap(received, "c"), bit_of("c"), 0).reshape(own.shape)
        return join(own, other, bit_of("x"), 0).reshape(-1, D).astype(F32)

    block_out, input_grad = (both_bins(own, r) for own, r in zip(finals, got))
    ends = [sum(sizes[: k + 1]) for k in range(4)]
    pieces = [flat[end - size : end] for end, size in zip(ends, sizes)]
    gains_sum = pieces[0].reshape(2, D)
    biases_sum = pieces[1].reshape(4, D)
    heads_sum = lax.dynamic_index_in_dim(
        pieces[2].reshape(2, 2, heads_each), x_index, 1, keepdims=False
    )
    units_sum = lax.dynamic_index_in_dim(pieces[3].reshape(2, units_each), x_index, 0, False)
    next_moments = (*narrow_nexts, *wide_nexts)
    returned = [back[owners[k]][:, : next_moments[k].shape[1]] for k in range(6)]
    keep_share = 1.0 - RATE * DECAY
    up_factor = math.sqrt(max(1.0, FF / D))
    qkv_next = qkv_weight.astype(F32) * keep_share - RATE * jnp.stack(returned[:3])
    out_next = out_weight.astype(F32) * keep_share - RATE * returned[3].T
    up_next = up_weight.astype(F32) * keep_share - RATE * up_factor * returned[4]
    down_next = down_weight.astype(F32) * keep_share - RATE * returned[5].T
    rate_vector = VECTOR_RATE / math.sqrt(groups * tokens.shape[0])
    gain_moment_next = MOMENTUM * gain_moment + gains_sum
    bias_moment_next = MOMENTUM * bias_moment + biases_sum
    head_moment_next = MOMENTUM * head_moment + heads_sum
    unit_moment_next = MOMENTUM * unit_moment + units_sum
    gain_next = norm_gains - rate_vector * gain_moment_next
    bias_next = shared_biases - rate_vector * bias_moment_next
    head_next = head_biases - rate_vector * head_moment_next
    unit_next = unit_bias - rate_vector * unit_moment_next
    return (
        block_out,
        input_grad,
        jnp.stack(next_moments[:3]),
        qkv_next,
        next_moments[3].T,
        out_next,
        next_moments[4],
        up_next,
        next_moments[5].T,
        down_next,
        gain_moment_next,
        gain_next,
        bias_moment_next,
        bias_next,
        head_moment_next,
        head_next,
        unit_moment_next,
        unit_next,
    )


def solution(mesh):
    dp_size, mp_size = mesh.devices.shape
    split = Mesh(
        mesh.devices.reshape(dp_size // 2, 2, mp_size // 2, 2), ("z", "y", "x", "c")
    )
    dp, mp = ("z", "y"), ("x", "c")
    in_specs = (
        P(dp, None),
        P(dp, None),
        P(),
        P(),
        P(None, dp, mp),
        P(mp, dp),
        P(dp, mp),
        P(mp, dp),
        P(),
        P(),
        P(None, mp),
        P(mp),
        P(None, dp, mp),
        P(mp, dp),
        P(dp, mp),
        P(mp, dp),
        P(),
        P(),
        P(None, mp),
        P(mp),
    )
    out_specs = (
        P(dp, None),
        P(dp, None),
        P(None, dp, mp),
        P(None, dp, mp),
        P(mp, dp),
        P(mp, dp),
        P(dp, mp),
        P(dp, mp),
        P(mp, dp),
        P(mp, dp),
        P(),
        P(),
        P(),
        P(),
        P(None, mp),
        P(None, mp),
        P(mp),
        P(mp),
    )
    return jax.shard_map(
        on_device, mesh=split, in_specs=in_specs, out_specs=out_specs, check_vma=False
    )
```

profile of v0, /device:TPU:0, one launch (start us, length us, event | category | flops | bytes accessed | tf_op | source)
XLA Modules:
  0.0 473.9 jit_solution(1588327330518132479)
XLA Ops:
  3.0 4.0 collective-permute-start
  23.0 3.4 collective-permute-start.3
  38.8 7.0 %collective-permute-done.2 = bf16[2,2,96,576]{3,2,0,1:T(8,128)(2,1)S(1)} collective-permute-done((bf16[2,2,96,576]{3,2,0,1:T(8,128)(2,1)S(1)}, bf16[2,2,96,576]{3,2,0,1:T(8,128)(2,1)S(1)}, u32[]{:S(2)}, u32[]{:S(2)}) %collective-permute-start.2) | collective-permute-done | bytes 442400 | tf_op jit(solution)/shard_map/ppermute | solution.py:35
  49.9 3.1 collective-permute-done.6
  62.0 6.2 %shard_map.340 = (bf16[1024,192]{1,0:T(8,128)(2,1)S(1)}, f32[1024,192]{1,0:T(8,128)S(1)}) custom-call(s32[1024,1]{1,0:T(8,128)S(1)} %select_select_fusion.low_ref, bf16[1024,576]{1,0:T(8,128)(2,1)S(1)} %multiply_convert_fusion.3.qkv_ref), custom_call_target="tpu_custom_call" | custom-call | flops 3221225472 | bytes 2363392 | tf_op jit(solution)/shard_map/pallas_call | solution.py:216
  68.2 3.4 collective-permute-done.7
  79.9 3.3 collective-permute-done.8
  83.2 2.8 multiply_convert_fusion.2.qkv_ref
  86.0 6.5 %shard_map.341 = (bf16[1024,192]{1,0:T(8,128)(2,1)S(1)}, f32[1024,192]{1,0:T(8,128)S(1)}) custom-call(s32[1024,1]{1,0:T(8,128)S(1)} %select_select_fusion.low_ref, bf16[1024,576]{1,0:T(8,128)(2,1)S(1)} %multiply_convert_fusion.2.qkv_ref), custom_call_target="tpu_custom_call" | custom-call | flops 3221225472 | bytes 2363392 | tf_op jit(solution)/shard_map/pallas_call | solution.py:216
  104.1 19.6 %collective-permute-done.14 = bf16[768,768]{1,0:T(8,128)(2,1)} collective-permute-done((bf16[768,768]{1,0:T(8,128)(2,1)}, bf16[768,768]{1,0:T(8,128)(2,1)}, u32[]{:S(2)}, u32[]{:S(2)}) %collective-permute-start.14) | collective-permute-done | bytes 1179680 | tf_op jit(solution)/shard_map/ppermute | solution.py:35
  126.4 3.7 multiply_convert_fusion.1
  130.2 3.3 multiply_convert_fusion
  133.4 3.5 convert_reduce_fusion.3
  137.0 3.7 convert_reduce_fusion.2
  140.7 3.2 fusion.99
  144.0 2.7 add_convert_fusion.1
  159.5 3.6 convolution_convert_fusion
  165.6 3.4 multiply_reduce_fusion
  169.1 3.9 fusion.84
  176.8 10.6 %shard_map.342 = bf16[1024,576]{1,0:T(8,128)(2,1)S(1)} custom-call(s32[1024,1]{1,0:T(8,128)S(1)} %select_select_fusion.low_ref, bf16[1024,576]{1,0:T(8,128)(2,1)} %copy-done.2, bf16[1024,192]{1,0:T(8,128)(2,1)S(1)} %convolution_convert_fusion.7.grad_ref, f32[1024,192]{1,0:T(8,128)S(1)} %copy-done.7), custom_call_target="tpu_custom_call" | custom-call | flops 8053063680 | bytes 3543040 | tf_op jit(solution)/shard_map/pallas_call | solution.py:216
  187.7 2.6 convolution_convert_fusion.5
  197.8 3.3 add_add_fusion.3
  207.0 18.4 %collective-permute-done.20 = bf16[768,960]{0,1:T(8,128)(2,1)S(1)} collective-permute-done((bf16[768,960]{0,1:T(8,128)(2,1)S(1)}, bf16[768,960]{0,1:T(8,128)(2,1)S(1)}, u32[]{:S(2)}, u32[]{:S(2)}) %collective-permute-start.20) | collective-permute-done | bytes 1474592 | tf_op jit(solution)/shard_map/ppermute | solution.py:35
  227.5 3.5 copy.108
  234.7 10.5 %shard_map.343 = bf16[1024,576]{1,0:T(8,128)(2,1)S(1)} custom-call(s32[1024,1]{1,0:T(8,128)S(1)} %select_select_fusion.low_ref, bf16[1024,576]{1,0:T(8,128)(2,1)} %copy-done.3, bf16[1024,192]{1,0:T(8,128)(2,1)S(1)} %copy-done.1, f32[1024,192]{1,0:T(8,128)S(1)} %copy-done.5), custom_call_target="tpu_custom_call" | custom-call | flops 8053063680 | bytes 3543040 | tf_op jit(solution)/shard_map/pallas_call | solution.py:216
  253.4 3.0 add_convert_fusion
  262.9 2.8 copy.118
  271.0 3.1 collective-permute-done.24
  275.4 3.6 collective-permute-done.29
  280.0 6.3 %collective-permute-done.27 = bf16[96,960]{1,0:T(8,128)(2,1)S(1)} collective-permute-done((bf16[96,960]{1,0:T(8,128)(2,1)S(1)}, bf16[96,960]{1,0:T(8,128)(2,1)S(1)}, u32[]{:S(2)}, u32[]{:S(2)}) %collective-permute-start.27) | collective-permute-done | bytes 184352 | tf_op jit(solution)/shard_map/ppermute | solution.py:35
  289.2 4.3 all-to-all-start
  294.0 3.9 fusion.24
  302.8 16.5 %collective-permute-done.30 = bf16[2,96,576]{2,1,0:T(8,128)(2,1)S(1)} collective-permute-done((bf16[2,96,576]{2,1,0:T(8,128)(2,1)S(1)}, bf16[2,96,576]{2,1,0:T(8,128)(2,1)S(1)}, u32[]{:S(2)}, u32[]{:S(2)}) %collective-permute-start.30) | collective-permute-done | bytes 221216 | tf_op jit(solution)/shard_map/ppermute | solution.py:35
  319.4 3.7 collective-permute-start.33
  323.1 2.7 fusion.100
  333.4 4.5 all-to-all-start.1
  342.1 7.5 %all-to-all-done.1 = bf16[8,96,192]{2,1,0:T(8,128)(2,1)S(1)} async-done(((bf16[8,96,192]{2,1,0:T(8,128)(2,1)}), bf16[8,96,192]{2,1,0:T(8,128)(2,1)S(1)}, u32[]{:S(2)}, u32[]{:S(2)}) %all-to-all-start.1) | async-done | bytes 294944 | tf_op jit(solution)/shard_map/all_to_all | solution.py:573
  353.3 3.8 fusion.82
  357.1 4.6 collective-permute-done.36
  364.3 10.1 %collective-permute-done.34 = f32[192,768]{1,0:T(8,128)S(1)} collective-permute-done((f32[192,768]{1,0:T(8,128)}, f32[192,768]{1,0:T(8,128)S(1)}, u32[]{:S(2)}, u32[]{:S(2)}) %collective-permute-start.34) | collective-permute-done | bytes 589856 | tf_op jit(solution)/shard_map/ppermute | solution.py:35
  374.3 8.9 %collective-permute-done.35 = f32[192,768]{1,0:T(8,128)S(1)} collective-permute-done((f32[192,768]{1,0:T(8,128)}, f32[192,768]{1,0:T(8,128)S(1)}, u32[]{:S(2)}, u32[]{:S(2)}) %collective-permute-start.35) | collective-permute-done | bytes 589856 | tf_op jit(solution)/shard_map/ppermute | solution.py:35
  397.2 18.5 %shard_map.344 = bf16[768,768]{1,0:T(8,128)(2,1)} custom-call(s32[1]{0:T(128)} %bitcast.86.wide_ref, f32[1]{0:T(128)} %bitcast.89.factor_ref, f32[20]{0:T(128)S(1)} %copy-done, f32[768,768]{1,0:T(8,128)} %bitcast.391, bf16[768,768]{1,0:T(8,128)(2,1)S(1)} %get-tuple-element.268.panel_ref), custom_call_target="tpu_custom_call" | custom-call | flops 22649241600 | bytes 5242880 | tf_op jit(solution)/shard_map/pallas_call | solution.py:352
  415.7 8.4 %collective-permute-done.42 = bf16[512,768]{1,0:T(8,128)(2,1)} collective-permute-done((bf16[512,768]{1,0:T(8,128)(2,1)}, bf16[512,768]{1,0:T(8,128)(2,1)}, u32[]{:S(2)}, u32[]{:S(2)}) %collective-permute-start.42) | collective-permute-done | bytes 786464 | tf_op jit(solution)/shard_map/ppermute | solution.py:35
  424.1 3.0 collective-permute-start.48
  430.6 8.1 %collective-permute-start.49 = (f32[54,128]{1,0:T(8,128)}, f32[54,128]{1,0:T(8,128)}, u32[]{:S(2)}, u32[]{:S(2)}) collective-permute-start(f32[54,128]{1,0:T(8,128)} %add.432), channel_id=1, source_target_pairs={{0,8},{8,0},{16,24},{24,16},{1,9},{9,1},{17,25},{25,17},{2,10},{10... | collective-permute-start | bytes 82952 | tf_op jit(solution)/shard_map/ppermute | solution.py:35
  440.4 3.6 all-to-all-start.2
  461.4 3.4 bitcast_convert_fusion
  464.8 3.4 bitcast_convert_fusion.1
  (495 shorter events, 192.5 us)
Async XLA Ops:
  3.0 10.3 %collective-permute-start = (bf16[96,576]{1,0:T(8,128)(2,1)}, bf16[96,576]{1,0:T(8,128)(2,1)}, u32[]{:S(2)}, u32[]{:S(2)}) collective-permute-start(bf16[96,576]{1,0:T(8,128)(2,1)} %pad_maximum_fusion.25), channel_id=1, source_target_pairs={{0,16},{8,24},{16,0},{24,8},{1,17},{9,25},{17,1},{25,9},{2,18},{10... | collective-permute-start | bytes 331784 | tf_op jit(solution)/shard_map/ppermute | solution.py:35
  17.2 13.2 %collective-permute-start.10 = (f32[1152]{0:T(1024)}, f32[1152]{0:T(1024)}, u32[]{:S(2)}, u32[]{:S(2)}) collective-permute-start(f32[1152]{0:T(1024)} %pad_maximum_fusion.27), channel_id=1, source_target_pairs={{0,2},{2,0},{1,3},{3,1},{4,6},{6,4},{5,7},{7,5},{8,10},{10,8},{9,1... | collective-permute-start | bytes 13832 | tf_op jit(solution)/shard_map/ppermute | solution.py:35
  18.7 13.9 %collective-permute-start.1 = (bf16[2,96,576]{2,1,0:T(8,128)(2,1)}, bf16[2,96,576]{2,1,0:T(8,128)(2,1)}, u32[]{:S(2)}, u32[]{:S(2)}) collective-permute-start(bf16[2,96,576]{2,1,0:T(8,128)(2,1)} %pad_maximum_fusion.23), channel_id=1, source_target_pairs={{0,8},{8,0},{16,24},{24,16},{1,9},{9,1},{17,25},{25,17},{2,10},{10... | collective-permute-start | bytes 663560 | tf_op jit(solution)/shard_map/ppermute | solution.py:35
  22.4 13.0 %collective-permute-start.4 = (bf16[96,768]{1,0:T(8,128)(2,1)S(1)}, bf16[96,768]{1,0:T(8,128)(2,1)S(1)}, u32[]{:S(2)}, u32[]{:S(2)}) collective-permute-start(bf16[96,768]{1,0:T(8,128)(2,1)S(1)} %bitcast.392), channel_id=1, source_target_pairs={{0,2},{2,0},{1,3},{3,1},{4,6},{6,4},{5,7},{7,5},{8,10},{10,8},{9,1... | collective-permute-start | bytes 442376 | tf_op jit(solution)/shard_map/ppermute | solution.py:35
  23.0 12.4 %collective-permute-start.3 = (bf16[96,960]{1,0:T(8,128)(2,1)S(1)}, bf16[96,960]{1,0:T(8,128)(2,1)S(1)}, u32[]{:S(2)}, u32[]{:S(2)}) collective-permute-start(bf16[96,960]{1,0:T(8,128)(2,1)S(1)} %pad_maximum_fusion.24), channel_id=1, source_target_pairs={{0,16},{8,24},{16,0},{24,8},{1,17},{9,25},{17,1},{25,9},{2,18},{10... | collective-permute-start | bytes 552968 | tf_op jit(solution)/shard_map/ppermute | solution.py:35
  33.8 12.1 %collective-permute-start.2 = (bf16[2,2,96,576]{3,2,0,1:T(8,128)(2,1)S(1)}, bf16[2,2,96,576]{3,2,0,1:T(8,128)(2,1)S(1)}, u32[]{:S(2)}, u32[]{:S(2)}) collective-permute-start(bf16[2,2,96,576]{3,2,0,1:T(8,128)(2,1)S(1)} %pad_maximum_fusion.19), channel_id=1, source_target_pairs={{0,4},{4,0},{1,5},{5,1},{2,6},{6,2},{3,7},{7,3},{8,12},{12,8},{9,1... | collective-permute-start | bytes 1327112 | tf_op jit(solution)/shard_map/ppermute | solution.py:35
  36.1 23.1 %collective-permute-start.5 = (bf16[2,96,768]{2,1,0:T(8,128)(2,1)}, bf16[2,96,768]{2,1,0:T(8,128)(2,1)}, u32[]{:S(2)}, u32[]{:S(2)}) collective-permute-start(bf16[2,96,768]{2,1,0:T(8,128)(2,1)} %pad_maximum_fusion.21), channel_id=1, source_target_pairs={{0,16},{8,24},{16,0},{24,8},{1,17},{9,25},{17,1},{25,9},{2,18},{10... | collective-permute-start | bytes 884744 | tf_op jit(solution)/shard_map/ppermute | solution.py:35
  36.3 16.7 %collective-permute-start.6 = (bf16[2,96,960]{2,1,0:T(8,128)(2,1)S(1)}, bf16[2,96,960]{2,1,0:T(8,128)(2,1)S(1)}, u32[]{:S(2)}, u32[]{:S(2)}) collective-permute-start(bf16[2,96,960]{2,1,0:T(8,128)(2,1)S(1)} %pad_maximum_fusion.20), channel_id=1, source_target_pairs={{0,8},{8,0},{16,24},{24,16},{1,9},{9,1},{17,25},{25,17},{2,10},{10... | collective-permute-start | bytes 1105928 | tf_op jit(solution)/shard_map/ppermute | solution.py:35
  54.1 17.5 %collective-permute-start.7 = (bf16[2,2,96,960]{3,2,0,1:T(8,128)(2,1)}, bf16[2,2,96,960]{3,2,0,1:T(8,128)(2,1)}, u32[]{:S(2)}, u32[]{:S(2)}) collective-permute-start(bf16[2,2,96,960]{3,2,0,1:T(8,128)(2,1)} %pad_maximum_fusion.16), channel_id=1, source_target_pairs={{0,4},{4,0},{1,5},{5,1},{2,6},{6,2},{3,7},{7,3},{8,12},{12,8},{9,1... | collective-permute-start | bytes 2211848 | tf_op jit(solution)/shard_map/ppermute | solution.py:35
  60.4 15.6 %collective-permute-start.9 = (bf16[2,2,96,768]{3,2,1,0:T(8,128)(2,1)S(1)}, bf16[2,2,96,768]{3,2,1,0:T(8,128)(2,1)S(1)}, u32[]{:S(2)}, u32[]{:S(2)}) collective-permute-start(bf16[2,2,96,768]{3,2,1,0:T(8,128)(2,1)S(1)} %pad_maximum_fusion.17), channel_id=1, source_target_pairs={{0,8},{8,0},{16,24},{24,16},{1,9},{9,1},{17,25},{25,17},{2,10},{10... | collective-permute-start | bytes 1769480 | tf_op jit(solution)/shard_map/ppermute | solution.py:35
  60.5 22.8 %collective-permute-start.8 = (bf16[768,576]{0,1:T(8,128)(2,1)S(1)}, bf16[768,576]{0,1:T(8,128)(2,1)}, u32[]{:S(2)}, u32[]{:S(2)}) collective-permute-start(bf16[768,576]{0,1:T(8,128)(2,1)S(1)} %copy-done.65), channel_id=1, source_target_pairs={{0,2},{2,0},{1,3},{3,1},{4,6},{6,4},{5,7},{7,5},{8,10},{10,8},{9,1... | collective-permute-start | bytes 2654216 | tf_op jit(solution)/shard_map/ppermute | solution.py:35
  74.5 18.0 %collective-permute-start.11 = (bf16[768,192]{1,0:T(8,128)(2,1)S(1)}, bf16[768,192]{1,0:T(8,128)(2,1)S(1)}, u32[]{:S(2)}, u32[]{:S(2)}) collective-permute-start(bf16[768,192]{1,0:T(8,128)(2,1)S(1)} %slice.453), channel_id=1, source_target_pairs={{0,2},{2,0},{1,3},{3,1},{4,6},{6,4},{5,7},{7,5},{8,10},{10,8},{9,1... | collective-permute-start | bytes 884744 | tf_op jit(solution)/shard_map/ppermute | solution.py:35
  77.4 25.0 %collective-permute-start.15 = (bf16[2,2,2,96,768]{4,3,2,1,0:T(8,128)(2,1)}, bf16[2,2,2,96,768]{4,3,2,1,0:T(8,128)(2,1)}, u32[]{:S(2)}, u32[]{:S(2)}) collective-permute-start(bf16[2,2,2,96,768]{4,3,2,1,0:T(8,128)(2,1)} %pad_maximum_fusion.11), channel_id=1, source_target_pairs={{0,4},{4,0},{1,5},{5,1},{2,6},{6,2},{3,7},{7,3},{8,12},{12,8},{9,1... | collective-permute-start | bytes 3538952 | tf_op jit(solution)/shard_map/ppermute | solution.py:35
  95.5 28.2 %collective-permute-start.14 = (bf16[768,768]{1,0:T(8,128)(2,1)}, bf16[768,768]{1,0:T(8,128)(2,1)}, u32[]{:S(2)}, u32[]{:S(2)}) collective-permute-start(bf16[768,768]{1,0:T(8,128)(2,1)} %slice.454), channel_id=1, source_target_pairs={{0,2},{2,0},{1,3},{3,1},{4,6},{6,4},{5,7},{7,5},{8,10},{10,8},{9,1... | collective-permute-start | bytes 3538952 | tf_op jit(solution)/shard_map/ppermute | solution.py:35
  154.0 47.1 %collective-permute-start.21 = (bf16[2,4,96,768]{3,2,1,0:T(8,128)(2,1)}, bf16[2,4,96,768]{3,2,1,0:T(8,128)(2,1)}, u32[]{:S(2)}, u32[]{:S(2)}) collective-permute-start(bf16[2,4,96,768]{3,2,1,0:T(8,128)(2,1)} %select_bitcast_fusion.2), channel_id=1, source_target_pairs={{0,4},{4,0},{1,5},{5,1},{2,6},{6,2},{3,7},{7,3},{8,12},{12,8},{9,1... | collective-permute-start | bytes 3538952 | tf_op jit(solution)/shard_map/ppermute | solution.py:35
  154.5 11.1 %collective-permute-start.18 = (bf16[512,768]{1,0:T(8,128)(2,1)}, bf16[512,768]{1,0:T(8,128)(2,1)}, u32[]{:S(2)}, u32[]{:S(2)}) collective-permute-start(bf16[512,768]{1,0:T(8,128)(2,1)} %get-tuple-element.305), channel_id=1, source_target_pairs={{0,1},{1,0},{2,3},{3,2},{4,5},{5,4},{6,7},{7,6},{8,9},{9,8},{10,11... | collective-permute-start | bytes 2359304 | tf_op jit(solution)/shard_map/ppermute | solution.py:35
  154.5 11.1 %collective-permute-start.19 = (bf16[512,768]{1,0:T(8,128)(2,1)}, bf16[512,768]{1,0:T(8,128)(2,1)}, u32[]{:S(2)}, u32[]{:S(2)}) collective-permute-start(bf16[512,768]{1,0:T(8,128)(2,1)} %get-tuple-element.306), channel_id=1, source_target_pairs={{0,1},{1,0},{2,3},{3,2},{4,5},{5,4},{6,7},{7,6},{8,9},{9,8},{10,11... | collective-permute-start | bytes 2359304 | tf_op jit(solution)/shard_map/ppermute | solution.py:35
  159.0 38.7 %collective-permute-start.16 = (bf16[512,768]{1,0:T(8,128)(2,1)}, bf16[512,768]{1,0:T(8,128)(2,1)}, u32[]{:S(2)}, u32[]{:S(2)}) collective-permute-start(bf16[512,768]{1,0:T(8,128)(2,1)} %get-tuple-element.307), channel_id=1, source_target_pairs={{0,1},{1,0},{2,3},{3,2},{4,5},{5,4},{6,7},{7,6},{8,9},{9,8},{10,11... | collective-permute-start | bytes 2359304 | tf_op jit(solution)/shard_map/ppermute | solution.py:35
  159.1 38.6 %collective-permute-start.17 = (bf16[512,768]{1,0:T(8,128)(2,1)}, bf16[512,768]{1,0:T(8,128)(2,1)}, u32[]{:S(2)}, u32[]{:S(2)}) collective-permute-start(bf16[512,768]{1,0:T(8,128)(2,1)} %get-tuple-element.308), channel_id=1, source_target_pairs={{0,1},{1,0},{2,3},{3,2},{4,5},{5,4},{6,7},{7,6},{8,9},{9,8},{10,11... | collective-permute-start | bytes 2359304 | tf_op jit(solution)/shard_map/ppermute | solution.py:35
  190.3 35.2 %collective-permute-start.20 = (bf16[768,960]{0,1:T(8,128)(2,1)S(1)}, bf16[768,960]{0,1:T(8,128)(2,1)S(1)}, u32[]{:S(2)}, u32[]{:S(2)}) collective-permute-start(bf16[768,960]{0,1:T(8,128)(2,1)S(1)} %pad_maximum_fusion.8), channel_id=1, source_target_pairs={{0,2},{2,0},{1,3},{3,1},{4,6},{6,4},{5,7},{7,5},{8,10},{10,8},{9,1... | collective-permute-start | bytes 4423688 | tf_op jit(solution)/shard_map/ppermute | solution.py:35
  194.1 66.1 %collective-permute-start.26 = (bf16[768,576]{0,1:T(8,128)(2,1)}, bf16[768,576]{0,1:T(8,128)(2,1)}, u32[]{:S(2)}, u32[]{:S(2)}) collective-permute-start(bf16[768,576]{0,1:T(8,128)(2,1)} %convolution_convert_fusion.5), channel_id=1, source_target_pairs={{0,2},{2,0},{1,3},{3,1},{4,6},{6,4},{5,7},{7,5},{8,10},{10,8},{9,1... | collective-permute-start | bytes 2654216 | tf_op jit(solution)/shard_map/ppermute | solution.py:35
  205.1 43.6 %collective-permute-start.23 = (bf16[2,2,96,768]{3,2,1,0:T(8,128)(2,1)}, bf16[2,2,96,768]{3,2,1,0:T(8,128)(2,1)}, u32[]{:S(2)}, u32[]{:S(2)}) collective-permute-start(bf16[2,2,96,768]{3,2,1,0:T(8,128)(2,1)} %fusion.35), channel_id=1, source_target_pairs={{0,8},{8,0},{16,24},{24,16},{1,9},{9,1},{17,25},{25,17},{2,10},{10... | collective-permute-start | bytes 1769480 | tf_op jit(solution)/shard_map/ppermute | solution.py:35
  233.1 25.0 %collective-permute-start.22 = (bf16[4,96,960]{2,1,0:T(8,128)(2,1)S(1)}, bf16[4,96,960]{2,1,0:T(8,128)(2,1)S(1)}, u32[]{:S(2)}, u32[]{:S(2)}) collective-permute-start(bf16[4,96,960]{2,1,0:T(8,128)(2,1)S(1)} %fusion.34), channel_id=1, source_target_pairs={{0,4},{4,0},{1,5},{5,1},{2,6},{6,2},{3,7},{7,3},{8,12},{12,8},{9,1... | collective-permute-start | bytes 2211848 | tf_op jit(solution)/shard_map/ppermute | solution.py:35
  251.3 16.7 %collective-permute-start.25 = (bf16[2,96,768]{2,1,0:T(8,128)(2,1)}, bf16[2,96,768]{2,1,0:T(8,128)(2,1)}, u32[]{:S(2)}, u32[]{:S(2)}) collective-permute-start(bf16[2,96,768]{2,1,0:T(8,128)(2,1)} %fusion.41), channel_id=1, source_target_pairs={{0,16},{8,24},{16,0},{24,8},{1,17},{9,25},{17,1},{25,9},{2,18},{10... | collective-permute-start | bytes 884744 | tf_op jit(solution)/shard_map/ppermute | solution.py:35
  257.6 36.3 %collective-permute-start.38 = (bf16[512,768]{1,0:T(8,128)(2,1)}, bf16[512,768]{1,0:T(8,128)(2,1)}, u32[]{:S(2)}, u32[]{:S(2)}) collective-permute-start(bf16[512,768]{1,0:T(8,128)(2,1)} %get-tuple-element.303), channel_id=1, source_target_pairs={{0,1},{1,0},{2,3},{3,2},{4,5},{5,4},{6,7},{7,6},{8,9},{9,8},{10,11... | collective-permute-start | bytes 2359304 | tf_op jit(solution)/shard_map/ppermute | solution.py:35
  257.6 36.3 %collective-permute-start.39 = (bf16[512,768]{1,0:T(8,128)(2,1)}, bf16[512,768]{1,0:T(8,128)(2,1)}, u32[]{:S(2)}, u32[]{:S(2)}) collective-permute-start(bf16[512,768]{1,0:T(8,128)(2,1)} %get-tuple-element.304), channel_id=1, source_target_pairs={{0,1},{1,0},{2,3},{3,2},{4,5},{5,4},{6,7},{7,6},{8,9},{9,8},{10,11... | collective-permute-start | bytes 2359304 | tf_op jit(solution)/shard_map/ppermute | solution.py:35
  259.9 14.2 %collective-permute-start.24 = (bf16[2,96,960]{2,1,0:T(8,128)(2,1)S(1)}, bf16[2,96,960]{2,1,0:T(8,128)(2,1)}, u32[]{:S(2)}, u32[]{:S(2)}) collective-permute-start(bf16[2,96,960]{2,1,0:T(8,128)(2,1)S(1)} %fusion.40), channel_id=1, source_target_pairs={{0,8},{8,0},{16,24},{24,16},{1,9},{9,1},{17,25},{25,17},{2,10},{10... | collective-permute-start | bytes 1105928 | tf_op jit(solution)/shard_map/ppermute | solution.py:35
  267.3 11.7 %collective-permute-start.29 = (bf16[4,96,576]{2,1,0:T(8,128)(2,1)S(1)}, bf16[4,96,576]{2,1,0:T(8,128)(2,1)S(1)}, u32[]{:S(2)}, u32[]{:S(2)}) collective-permute-start(bf16[4,96,576]{2,1,0:T(8,128)(2,1)S(1)} %fusion.39), channel_id=1, source_target_pairs={{0,4},{4,0},{1,5},{5,1},{2,6},{6,2},{3,7},{7,3},{8,12},{12,8},{9,1... | collective-permute-start | bytes 1327112 | tf_op jit(solution)/shard_map/ppermute | solution.py:35
  269.5 10.5 %collective-permute-start.28 = (bf16[96,768]{1,0:T(8,128)(2,1)S(1)}, bf16[96,768]{1,0:T(8,128)(2,1)S(1)}, u32[]{:S(2)}, u32[]{:S(2)}) collective-permute-start(bf16[96,768]{1,0:T(8,128)(2,1)S(1)} %fusion.51), channel_id=1, source_target_pairs={{0,2},{2,0},{1,3},{3,1},{4,6},{6,4},{5,7},{7,5},{8,10},{10,8},{9,1... | collective-permute-start | bytes 442376 | tf_op jit(solution)/shard_map/ppermute | solution.py:35
  275.3 11.1 %collective-permute-start.27 = (bf16[96,960]{1,0:T(8,128)(2,1)S(1)}, bf16[96,960]{1,0:T(8,128)(2,1)S(1)}, u32[]{:S(2)}, u32[]{:S(2)}) collective-permute-start(bf16[96,960]{1,0:T(8,128)(2,1)S(1)} %fusion.47), channel_id=1, source_target_pairs={{0,16},{8,24},{16,0},{24,8},{1,17},{9,25},{17,1},{25,9},{2,18},{10... | collective-permute-start | bytes 552968 | tf_op jit(solution)/shard_map/ppermute | solution.py:35
  289.2 33.9 %all-to-all-start = ((bf16[8,96,768]{2,1,0:T(8,128)(2,1)}), bf16[8,96,768]{2,1,0:T(8,128)(2,1)}, u32[]{:S(2)}, u32[]{:S(2)}) async-start(bf16[8,96,768]{2,1,0:T(8,128)(2,1)} %copy-done.41), calls=%async_computation | async-start | bytes 2359296 | tf_op jit(solution)/shard_map/all_to_all | solution.py:573
  298.7 63.3 %collective-permute-start.40 = (f32[54,128]{1,0:T(8,128)}, f32[54,128]{1,0:T(8,128)}, u32[]{:S(2)}, u32[]{:S(2)}) collective-permute-start(f32[54,128]{1,0:T(8,128)} %maximum_bitcast_fusion), channel_id=1, source_target_pairs={{0,2},{2,0},{1,3},{3,1},{4,6},{6,4},{5,7},{7,5},{8,10},{10,8},{9,1... | collective-permute-start | bytes 82952 | tf_op jit(solution)/shard_map/ppermute | solution.py:35
  300.3 19.0 %collective-permute-start.30 = (bf16[2,96,576]{2,1,0:T(8,128)(2,1)S(1)}, bf16[2,96,576]{2,1,0:T(8,128)(2,1)S(1)}, u32[]{:S(2)}, u32[]{:S(2)}) collective-permute-start(bf16[2,96,576]{2,1,0:T(8,128)(2,1)S(1)} %copy-done.75), channel_id=1, source_target_pairs={{0,8},{8,0},{16,24},{24,16},{1,9},{9,1},{17,25},{25,17},{2,10},{10... | collective-permute-start | bytes 663560 | tf_op jit(solution)/shard_map/ppermute | solution.py:35
  319.4 9.0 %collective-permute-start.33 = (bf16[96,576]{1,0:T(8,128)(2,1)S(1)}, bf16[96,576]{1,0:T(8,128)(2,1)S(1)}, u32[]{:S(2)}, u32[]{:S(2)}) collective-permute-start(bf16[96,576]{1,0:T(8,128)(2,1)S(1)} %fusion.52), channel_id=1, source_target_pairs={{0,16},{8,24},{16,0},{24,8},{1,17},{9,25},{17,1},{25,9},{2,18},{10... | collective-permute-start | bytes 331784 | tf_op jit(solution)/shard_map/ppermute | solution.py:35
  330.0 7.9 %collective-permute-start.31 = (f32[192,768]{1,0:T(8,128)S(1)}, f32[192,768]{1,0:T(8,128)S(1)}, u32[]{:S(2)}, u32[]{:S(2)}) collective-permute-start(f32[192,768]{1,0:T(8,128)S(1)} %get-tuple-element.317), channel_id=1, source_target_pairs={{0,1},{1,0},{2,3},{3,2},{4,5},{5,4},{6,7},{7,6},{8,9},{9,8},{10,11... | collective-permute-start | bytes 1769480 | tf_op jit(solution)/shard_map/ppermute | solution.py:35
  330.0 7.9 %collective-permute-start.32 = (f32[192,768]{1,0:T(8,128)S(1)}, f32[192,768]{1,0:T(8,128)S(1)}, u32[]{:S(2)}, u32[]{:S(2)}) collective-permute-start(f32[192,768]{1,0:T(8,128)S(1)} %get-tuple-element.318), channel_id=1, source_target_pairs={{0,1},{1,0},{2,3},{3,2},{4,5},{5,4},{6,7},{7,6},{8,9},{9,8},{10,11... | collective-permute-start | bytes 1769480 | tf_op jit(solution)/shard_map/ppermute | solution.py:35
  333.4 16.3 %all-to-all-start.1 = ((bf16[8,96,192]{2,1,0:T(8,128)(2,1)}), bf16[8,96,192]{2,1,0:T(8,128)(2,1)S(1)}, u32[]{:S(2)}, u32[]{:S(2)}) async-start(bf16[8,96,192]{2,1,0:T(8,128)(2,1)} %fusion.60), calls=%async_computation.1 | async-start | bytes 786432 | tf_op jit(solution)/shard_map/all_to_all | solution.py:573
  349.6 12.1 %collective-permute-start.36 = (bf16[768,192]{1,0:T(8,128)(2,1)S(1)}, bf16[768,192]{1,0:T(8,128)(2,1)S(1)}, u32[]{:S(2)}, u32[]{:S(2)}) collective-permute-start(bf16[768,192]{1,0:T(8,128)(2,1)S(1)} %bitcast.388), channel_id=1, source_target_pairs={{0,2},{2,0},{1,3},{3,1},{4,6},{6,4},{5,7},{7,5},{8,10},{10,8},{9,1... | collective-permute-start | bytes 884744 | tf_op jit(solution)/shard_map/ppermute | solution.py:35
  351.2 23.1 %collective-permute-start.34 = (f32[192,768]{1,0:T(8,128)}, f32[192,768]{1,0:T(8,128)S(1)}, u32[]{:S(2)}, u32[]{:S(2)}) collective-permute-start(f32[192,768]{1,0:T(8,128)} %get-tuple-element.315), channel_id=1, source_target_pairs={{0,2},{2,0},{1,3},{3,1},{4,6},{6,4},{5,7},{7,5},{8,10},{10,8},{9,1... | collective-permute-start | bytes 1769480 | tf_op jit(solution)/shard_map/ppermute | solution.py:35
  351.7 31.6 %collective-permute-start.35 = (f32[192,768]{1,0:T(8,128)}, f32[192,768]{1,0:T(8,128)S(1)}, u32[]{:S(2)}, u32[]{:S(2)}) collective-permute-start(f32[192,768]{1,0:T(8,128)} %get-tuple-element.316), channel_id=1, source_target_pairs={{0,2},{2,0},{1,3},{3,1},{4,6},{6,4},{5,7},{7,5},{8,10},{10,8},{9,1... | collective-permute-start | bytes 1769480 | tf_op jit(solution)/shard_map/ppermute | solution.py:35
  361.9 21.4 %collective-permute-start.37 = (bf16[768,384]{1,0:T(8,128)(2,1)S(1)}, bf16[768,384]{1,0:T(8,128)(2,1)S(1)}, u32[]{:S(2)}, u32[]{:S(2)}) collective-permute-start(bf16[768,384]{1,0:T(8,128)(2,1)S(1)} %pad_maximum_fusion.18), channel_id=1, source_target_pairs={{0,1},{1,0},{2,3},{3,2},{4,5},{5,4},{6,7},{7,6},{8,9},{9,8},{10,11... | collective-permute-start | bytes 1769480 | tf_op jit(solution)/shard_map/ppermute | solution.py:35
  362.8 21.1 %collective-permute-start.41 = (f32[54,128]{1,0:T(8,128)S(1)}, f32[54,128]{1,0:T(8,128)S(1)}, u32[]{:S(2)}, u32[]{:S(2)}) collective-permute-start(f32[54,128]{1,0:T(8,128)S(1)} %fusion.142), channel_id=1, source_target_pairs={{0,4},{4,0},{1,5},{5,1},{2,6},{6,2},{3,7},{7,3},{8,12},{12,8},{9,1... | collective-permute-start | bytes 82952 | tf_op jit(solution)/shard_map/ppermute | solution.py:35
  388.6 27.1 %collective-permute-start.43 = (bf16[512,768]{1,0:T(8,128)(2,1)S(1)}, bf16[512,768]{1,0:T(8,128)(2,1)}, u32[]{:S(2)}, u32[]{:S(2)}) collective-permute-start(bf16[512,768]{1,0:T(8,128)(2,1)S(1)} %constant_dynamic-slice_fusion.1), channel_id=1, source_target_pairs={{0,2},{2,0},{1,3},{3,1},{4,6},{6,4},{5,7},{7,5},{8,10},{10,8},{9,1... | collective-permute-start | bytes 2359304 | tf_op jit(solution)/shard_map/ppermute | solution.py:35
  391.2 32.9 %collective-permute-start.42 = (bf16[512,768]{1,0:T(8,128)(2,1)}, bf16[512,768]{1,0:T(8,128)(2,1)}, u32[]{:S(2)}, u32[]{:S(2)}) collective-permute-start(bf16[512,768]{1,0:T(8,128)(2,1)} %constant_dynamic-slice_fusion.2), channel_id=1, source_target_pairs={{0,2},{2,0},{1,3},{3,1},{4,6},{6,4},{5,7},{7,5},{8,10},{10,8},{9,1... | collective-permute-start | bytes 2359304 | tf_op jit(solution)/shard_map/ppermute | solution.py:35
  430.6 13.9 %collective-permute-start.49 = (f32[54,128]{1,0:T(8,128)}, f32[54,128]{1,0:T(8,128)}, u32[]{:S(2)}, u32[]{:S(2)}) collective-permute-start(f32[54,128]{1,0:T(8,128)} %add.432), channel_id=1, source_target_pairs={{0,8},{8,0},{16,24},{24,16},{1,9},{9,1},{17,25},{25,17},{2,10},{10... | collective-permute-start | bytes 82952 | tf_op jit(solution)/shard_map/ppermute | solution.py:35
  440.4 29.9 %all-to-all-start.2 = ((bf16[8,96,768]{2,1,0:T(8,128)(2,1)}), bf16[8,96,768]{2,1,0:T(8,128)(2,1)S(1)}, u32[]{:S(2)}, u32[]{:S(2)}) async-start(bf16[8,96,768]{2,1,0:T(8,128)(2,1)} %bitcast.106), calls=%async_computation.2 | async-start | bytes 2359296 | tf_op jit(solution)/shard_map/all_to_all | solution.py:611
  443.9 11.9 %collective-permute-start.46 = (bf16[512,768]{1,0:T(8,128)(2,1)}, bf16[512,768]{1,0:T(8,128)(2,1)}, u32[]{:S(2)}, u32[]{:S(2)}) collective-permute-start(bf16[512,768]{1,0:T(8,128)(2,1)} %collective-permute-done.42), channel_id=1, source_target_pairs={{0,1},{1,0},{2,3},{3,2},{4,5},{5,4},{6,7},{7,6},{8,9},{9,8},{10,11... | collective-permute-start | bytes 2359304 | tf_op jit(solution)/shard_map/ppermute | solution.py:35
  444.0 14.1 %collective-permute-start.47 = (bf16[512,768]{1,0:T(8,128)(2,1)}, bf16[512,768]{1,0:T(8,128)(2,1)S(1)}, u32[]{:S(2)}, u32[]{:S(2)}) collective-permute-start(bf16[512,768]{1,0:T(8,128)(2,1)} %collective-permute-done.43), channel_id=1, source_target_pairs={{0,1},{1,0},{2,3},{3,2},{4,5},{5,4},{6,7},{7,6},{8,9},{9,8},{10,11... | collective-permute-start | bytes 2359304 | tf_op jit(solution)/shard_map/ppermute | solution.py:35
  (117 other events, 1701.7 us)
where the time goes:
time: 481 us; the launch traced here: 474 us
  waiting for transfers between devices  129 us (27%)
  other arithmetic  107 us (22%)
  starting transfers between devices  74.8 us (16%)
  matrix products  53.2 us (11%)
  local copies, waits for them, and re-layouts  52.9 us (11%)
  Pallas kernels  52.3 us (11%)
    ppermute x50, waiting for transfers between devices, swap(): return lax.ppermute(value, axis, [(i, i ^ distance) for i in range(size)])  120 us
    ppermute x50, starting transfers between devices, swap(): return lax.ppermute(value, axis, [(i, i ^ distance) for i in range(size)])  62.5 us
    pallas_call x4, Pallas kernels, on_chip(): pl.pallas_call(kernel, out_shape=shapes, in_specs=[pl.BlockSpec(memory_sp...  33.8 us
    unnamed x229, local copies, waits for them, and re-layouts  21 us
    pallas_call x1, Pallas kernels, newton(): pl.pallas_call(newton_kernel, out_shape=shape, in_specs=[scalar, scalar,...  18.5 us
    dot_general x9, matrix products, dot_nt(): lax.dot_general(left, right, (((1,), (1,)), ((), ())), preferred_element_...  17.2 us
    another operation x28, other arithmetic, join(): return jnp.stack((low, high), axis=dim)  16.1 us
    dot_general x8, matrix products, dot_tn(): lax.dot_general(left, right, (((0,), (0,)), ((), ())), preferred_element_...  14.5 us
  transfers between devices with their start and end apart: 53, of which 20 were waited for; matrix products, arithmetic and copies ran while one was open for 32% of the time, Pallas kernels for 11%

commit v1 on v0

--- a/solution.py
+++ b/solution.py
@@ -100,13 +100,6 @@
 
 def by_rows(grad):
     return grad.reshape(lax.axis_size("z"), 2, -1, grad.shape[-1])
-
-
-def all_sum(value, axes):
-    for axis in axes:
-        for distance in distances(axis):
-            value = value + swap(value, axis, distance)
-    return value
 
 
 def swap_cores(own):
@@ -211,8 +204,7 @@
         out_ref[:, value_lanes] = values_sum[...].astype(BF)
 
 
-def on_chip(kernel, shapes, scratch, flops, exps, *operands):
-    moved = sum(o.size * o.dtype.itemsize for o in (*operands, *shapes))
+def on_chip(kernel, shapes, scratch, *operands):
     return pl.pallas_call(
         kernel,
         out_shape=shapes,
@@ -220,7 +212,7 @@
         out_specs=[pl.BlockSpec(memory_space=pltpu.VMEM)] * len(shapes),
         scratch_shapes=scratch,
         compiler_params=pltpu.CompilerParams(vmem_limit_bytes=50 * 2**20),
-        cost_estimate=pl.CostEstimate(flops=flops, bytes_accessed=moved, transcendentals=exps),
+        cost_estimate=pl.CostEstimate(flops=0, bytes_accessed=0, transcendentals=0),
     )(*operands)
 
 
@@ -230,17 +222,13 @@
         jax.ShapeDtypeStruct((SLOTS, width), BF),
         jax.ShapeDtypeStruct((SLOTS, width), F32),
     ]
-    pairs = SLOTS * SLOTS * width // HEAD_DIM
-    return on_chip(attend_kernel, shapes, [], 16 * pairs * HEAD_DIM, pairs, low, qkv)
+    return on_chip(attend_kernel, shapes, [], low, qkv)
 
 
 def attend_back(low, qkv, grad, log_total):
     shapes = [jax.ShapeDtypeStruct(qkv.shape, BF)]
     scratch = [pltpu.VMEM((SLOTS, HEAD_DIM), F32)] * 2
-    pairs = SLOTS * SLOTS * grad.shape[1] // HEAD_DIM
-    return on_chip(
-        attend_back_kernel, shapes, scratch, 40 * pairs * HEAD_DIM, pairs, low, qkv, grad, log_total
-    )[0]
+    return on_chip(attend_back_kernel, shapes, scratch, low, qkv, grad, log_total)[0]
 
 
 def newton_kernel(
@@ -562,41 +550,80 @@
     )
     spread = groups // 8
     owners = [number * spread for number in (0, 3, 4, 7, 2, 5)]
-
-    def to_owners(numbers, grads):
+    planes_xy = ("z", "y")
+    everywhere = ("z", "y", "x")
+    chips = [owner * 2 + number % 2 for number, owner in enumerate(owners[:4])]
+
+    def updated(numbers, grads):
         nexts = [MOMENTUM * moments[k] + grad for k, grad in zip(numbers, grads)]
         panels = [(grad + MOMENTUM * m).astype(BF) for m, grad in zip(nexts, grads)]
+        return nexts, panels
+
+    def to_wide_owners(panels):
+        pieces = [jnp.where(position == owners[4], *panels)]
+        for k in range(1, groups):
+            pairs = [(owner ^ k, owner) for owner in owners[4:]]
+            sent = jnp.where(position == owners[4] ^ k, *panels)
+            pieces.append(lax.ppermute(sent, planes_xy, pairs))
+        return jnp.concatenate(pieces, axis=0)
+
+    def from_wide_owners(orth):
+        blocks = orth.reshape(groups, rows_each, -1)
+        found = [blocks[0], blocks[0]]
+        for k in range(1, groups):
+            pairs = [(owner, owner ^ k) for owner in owners[4:]]
+            got = lax.ppermute(blocks[k], planes_xy, pairs)
+            found = [
+                jnp.where(position == owner ^ k, got, value)
+                for owner, value in zip(owners[4:], found)
+            ]
+        return found
+
+    def to_square_owners(panels):
         width = panels[0].shape[1]
-        outgoing = jnp.zeros((groups, rows_each, width), BF)
-        for number, panel in zip(numbers, panels):
-            outgoing = outgoing.at[owners[number]].set(panel)
-        incoming = lax.all_to_all(outgoing, ("z", "y"), split_axis=0, concat_axis=0, tiled=True)
-        return nexts, incoming.reshape(groups * rows_each, width)
+        outgoing = jnp.zeros((2 * groups, rows_each, width), BF)
+        for chip, panel in zip(chips, panels):
+            outgoing = outgoing.at[chip].set(panel)
+        incoming = lax.all_to_all(outgoing, everywhere, split_axis=0, concat_axis=0, tiled=True)
+        incoming = incoming.reshape(groups, 2, rows_each, width)
+        return jnp.moveaxis(incoming, 1, 2).reshape(groups * rows_each, 2 * width)
+
+    def from_square_owners(orth):
+        width = heads_each
+        outgoing = orth[:, : 2 * width].reshape(groups, rows_each, 2, width)
+        outgoing = jnp.moveaxis(outgoing, 2, 1).reshape(2 * groups, rows_each, width)
+        back = lax.all_to_all(outgoing, everywhere, split_axis=0, concat_axis=0, tiled=True)
+        return [back[chip] for chip in chips]
 
     def swap_parts(value, axis):
         half = value.shape[0] // 2
         return jnp.concatenate((swap(value[:half], axis), swap(value[half:], axis)), axis=0)
 
-    wide_nexts, wide = to_owners((4, 5), (sum_up, sum_down))
-    last = wide
+    wide_nexts, wide_panels = updated((4, 5), (sum_up, sum_down))
+    wide = to_wide_owners(wide_panels)
+    last = wide_nexts[1]
     for lead in range(depth - 1, 0, -1):
-        square_offer = offer(settle(square_offer, wide_nexts[1]), "z", lead - 1, z_steps[lead - 1])
-        wide = after(wide, square_offer[1])
+        square_offer = offer(settle(square_offer, last), "z", lead - 1, z_steps[lead - 1])
+        last = square_offer[1]
+    wide = after(wide, last)
     gram = dot_nt(wide, wide).reshape(2, D // 2, D)
     keep, send = take(gram, bit_of("c"), 0)
     send = fixed32(send)
     gram_sent = swap_parts(send, "c")
     sum_square = settle(square_offer, send)
-    narrow_grads = [sum_square[:, k * heads_each : (k + 1) * heads_each] for k in range(3)]
-    narrow_nexts, narrow = to_owners((0, 1, 2, 3), (*narrow_grads, sum_out))
     gram = fixed32(keep + after(gram_sent, sum_square))
     gram_got = swap_parts(gram, "x")
-    narrow = after(narrow, gram)
-    pair = jnp.concatenate((narrow, swap(narrow, "x")), axis=1)
-    flat = flat + after(swap(flat, "x"), narrow)
-    pair = jnp.concatenate((pair, swap(pair, "c")), axis=1)
+    narrow_grads = [sum_square[:, k * heads_each : (k + 1) * heads_each] for k in range(3)]
+    narrow_nexts, narrow_panels = updated((0, 1, 2, 3), (*narrow_grads, sum_out))
+    narrow = to_square_owners(narrow_panels)
+    flat = flat + after(swap(flat, "x"), narrow_panels[0])
+    narrow = after(narrow, gram, flat)
+    pair = jnp.concatenate((narrow, swap(narrow, "c")), axis=1)
     flat = flat + after(swap(flat, "y"), pair)
     gram = gram + after(gram_got, pair, flat)
+    for distance in z_steps[:-1]:
+        flat = flat + after(swap(flat, "z", distance), gram)
+    flat_got = swap(flat, "z", z_steps[-1])
     half = SLOTS // 2
     core = lax.axis_index("c")
     finals = [fixed(after(result, gram)), fixed(after(grad_hidden + grad_source, gram))]
@@ -607,15 +634,10 @@
     norm = jnp.where(is_wide, jnp.trace(gram), jnp.sum(pair_values * pair_values))
     factor = 1.0 / (jnp.sqrt(norm) + 1e-07)
     orth = newton(is_wide, factor, gram, jnp.where(is_wide, wide, pair))
-    got, flat, back_sent = lax.optimization_barrier((got, flat, orth))
-    back = lax.all_to_all(
-        back_sent.reshape(groups, rows_each, units_each),
-        ("z", "y"),
-        split_axis=0,
-        concat_axis=0,
-        tiled=True,
-    ).astype(F32)
-    flat = all_sum(flat, ("z",)).reshape(-1)
+    got, flat_got, orth = lax.optimization_barrier((got, flat_got, orth))
+    wide_back = from_wide_owners(orth)
+    square_back = from_square_owners(orth)
+    flat = (flat + flat_got).reshape(-1)
 
     def both_bins(own, received):
         other = join(received, swap(received, "c"), bit_of("c"), 0).reshape(own.shape)
@@ -631,7 +653,7 @@
     )
     units_sum = lax.dynamic_index_in_dim(pieces[3].reshape(2, units_each), x_index, 0, False)
     next_moments = (*narrow_nexts, *wide_nexts)
-    returned = [back[owners[k]][:, : next_moments[k].shape[1]] for k in range(6)]
+    returned = [value.astype(F32) for value in (*square_back, *wide_back)]
     keep_share = 1.0 - RATE * DECAY
     up_factor = math.sqrt(max(1.0, FF / D))
     qkv_next = qkv_weight.astype(F32) * keep_share - RATE * jnp.stack(returned[:3])

time: 481 us -> 502 us (1.044)
  starting transfers between devices: 74.8 us -> 87.9 us
  local copies, waits for them, and re-layouts: 52.9 us -> 60.3 us
    ppermute x0 -> x14, starting transfers between devices: none -> 28.7 us  [the longest x7 22.7 us: to_wide_owners(): pieces.append(lax.ppermute(sent, planes_xy, pairs))]
    ppermute x50 -> x49, waiting for transfers between devices: 120 us -> 97.1 us  [swap(): return lax.ppermute(value, axis, [(i, i ^ distance) for i in range(size)])]
    ppermute x0 -> x14, waiting for transfers between devices: none -> 19.6 us  [the longest x7 15.9 us: from_wide_owners(): got = lax.ppermute(blocks[k], planes_xy, pairs)]
    ppermute x50 -> x49, starting transfers between devices: 62.5 us -> 47.2 us  [swap(): return lax.ppermute(value, axis, [(i, i ^ distance) for i in range(size)])]
    unnamed x229 -> x258, local copies, waits for them, and re-layouts: 21 us -> 23.1 us
    all_to_all x3 -> x2, starting transfers between devices: 12.3 us -> 12 us  [the longest x1 6.55 us: to_square_owners(): lax.all_to_all(outgoing, everywhere, split_axis=0, concat_axis=0, tiled=T...]
  transfers between devices with their start and end apart: 53 -> 65, of which waited for: 20 -> 17; matrix products, arithmetic and copies ran while one was open for 32% -> 33% of each run, Pallas kernels for 11% -> 10%
where the time goes in v1:
time: 502 us; the launch traced here: 492 us
  waiting for transfers between devices  126 us (25%)
  other arithmetic  107 us (21%)
  starting transfers between devices  87.9 us (18%)
  local copies, waits for them, and re-layouts  60.3 us (12%)
  matrix products  53.9 us (11%)
  Pallas kernels  51.2 us (10%)
    ppermute x49, waiting for transfers between devices, swap(): return lax.ppermute(value, axis, [(i, i ^ distance) for i in range(size)])  97.1 us
    ppermute x49, starting transfers between devices, swap(): return lax.ppermute(value, axis, [(i, i ^ distance) for i in range(size)])  47.2 us
    pallas_call x4, Pallas kernels, on_chip(): pl.pallas_call(kernel, out_shape=shapes, in_specs=[pl.BlockSpec(memory_sp...  33.8 us
    unnamed x258, local copies, waits for them, and re-layouts  23.1 us
    ppermute x7, starting transfers between devices, to_wide_owners(): pieces.append(lax.ppermute(sent, planes_xy, pairs))  22.7 us
    dot_general x9, matrix products, dot_nt(): lax.dot_general(left, right, (((1,), (1,)), ((), ())), preferred_element_...  17.8 us
    pallas_call x1, Pallas kernels, newton(): pl.pallas_call(newton_kernel, out_shape=shape, in_specs=[scalar, scalar,...  17.4 us
    another operation x28, other arithmetic, join(): return jnp.stack((low, high), axis=dim)  16.8 us
  transfers between devices with their start and end apart: 65, of which 17 were waited for; matrix products, arithmetic and copies ran while one was open for 33% of the time, Pallas kernels for 10%

profile of v1, /device:TPU:0, one launch (start us, length us, event | category | flops | bytes accessed | tf_op | source)
XLA Modules:
  0.0 492.0 jit_solution(14104223024446658037)
XLA Ops:
  1.8 4.1 collective-permute-start
  20.1 3.4 collective-permute-start.3
  27.8 4.2 collective-permute-done.3
  32.2 3.0 collective-permute-start.6
  35.2 3.0 collective-permute-done.2
  42.3 7.0 %collective-permute-done.6 = bf16[2,96,960]{2,1,0:T(8,128)(2,1)S(1)} collective-permute-done((bf16[2,96,960]{2,1,0:T(8,128)(2,1)S(1)}, bf16[2,96,960]{2,1,0:T(8,128)(2,1)S(1)}, u32[]{:S(2)}, u32[]{:S(2)}) %collective-permute-start.6) | collective-permute-done | bytes 368672 | tf_op jit(solution)/shard_map/ppermute | solution.py:35
  63.8 6.2 %shard_map.340 = (bf16[1024,192]{1,0:T(8,128)(2,1)S(1)}, f32[1024,192]{1,0:T(8,128)S(1)}) custom-call(s32[1024,1]{1,0:T(8,128)S(1)} %select_select_fusion.low_ref, bf16[1024,576]{1,0:T(8,128)(2,1)S(1)} %multiply_convert_fusion.3.qkv_ref), custom_call_target="tpu_custom_call" | custom-call | tf_op jit(solution)/shard_map/pallas_call | solution.py:208
  77.7 7.5 %collective-permute-done.8 = bf16[768,576]{0,1:T(8,128)(2,1)} collective-permute-done((bf16[768,576]{0,1:T(8,128)(2,1)}, bf16[768,576]{0,1:T(8,128)(2,1)}, u32[]{:S(2)}, u32[]{:S(2)}) %collective-permute-start.8) | collective-permute-done | bytes 884768 | tf_op jit(solution)/shard_map/ppermute | solution.py:35
  85.2 2.7 multiply_convert_fusion.2.qkv_ref
  88.0 6.5 %shard_map.341 = (bf16[1024,192]{1,0:T(8,128)(2,1)S(1)}, f32[1024,192]{1,0:T(8,128)S(1)}) custom-call(s32[1024,1]{1,0:T(8,128)S(1)} %select_select_fusion.low_ref, bf16[1024,576]{1,0:T(8,128)(2,1)S(1)} %multiply_convert_fusion.2.qkv_ref), custom_call_target="tpu_custom_call" | custom-call | tf_op jit(solution)/shard_map/pallas_call | solution.py:208
  106.8 19.3 %collective-permute-done.14 = bf16[768,768]{1,0:T(8,128)(2,1)} collective-permute-done((bf16[768,768]{1,0:T(8,128)(2,1)}, bf16[768,768]{1,0:T(8,128)(2,1)}, u32[]{:S(2)}, u32[]{:S(2)}) %collective-permute-start.14) | collective-permute-done | bytes 1179680 | tf_op jit(solution)/shard_map/ppermute | solution.py:35
  128.8 3.7 multiply_convert_fusion.1
  132.6 3.3 multiply_convert_fusion
  135.9 3.5 convert_reduce_fusion.3
  139.4 3.7 convert_reduce_fusion.2
  143.1 3.2 fusion.92
  146.4 2.7 add_convert_fusion.1
  162.7 3.6 convolution_convert_fusion
  171.2 2.9 fusion.75
  178.6 10.6 %shard_map.342 = bf16[1024,576]{1,0:T(8,128)(2,1)S(1)} custom-call(s32[1024,1]{1,0:T(8,128)S(1)} %select_select_fusion.low_ref, bf16[1024,576]{1,0:T(8,128)(2,1)} %copy-done.1, bf16[1024,192]{1,0:T(8,128)(2,1)S(1)} %convolution_convert_fusion.7.grad_ref, f32[1024,192]{1,0:T(8,128)S(1)} %copy-done.3), custom_call_target="tpu_custom_call" | custom-call | tf_op jit(solution)/shard_map/pallas_call | solution.py:208
  189.4 2.6 convolution_convert_fusion.5
  198.7 3.3 add_add_fusion.3
  207.8 19.4 %collective-permute-done.20 = bf16[768,960]{0,1:T(8,128)(2,1)S(1)} collective-permute-done((bf16[768,960]{0,1:T(8,128)(2,1)S(1)}, bf16[768,960]{0,1:T(8,128)(2,1)S(1)}, u32[]{:S(2)}, u32[]{:S(2)}) %collective-permute-start.20) | collective-permute-done | bytes 1474592 | tf_op jit(solution)/shard_map/ppermute | solution.py:35
  229.2 3.6 copy.106
  232.8 2.9 fusion.33
  237.2 10.5 %shard_map.343 = bf16[1024,576]{1,0:T(8,128)(2,1)S(1)} custom-call(s32[1024,1]{1,0:T(8,128)S(1)} %select_select_fusion.low_ref, bf16[1024,576]{1,0:T(8,128)(2,1)} %copy-done, bf16[1024,192]{1,0:T(8,128)(2,1)S(1)} %convolution_convert_fusion.6.grad_ref, f32[1024,192]{1,0:T(8,128)S(1)} %get-tuple-element.146.log_ref), custom_call_target="tpu_custom_call" | custom-call | tf_op jit(solution)/shard_map/pallas_call | solution.py:208
  248.0 3.1 fusion.94
  259.8 3.6 add_convert_fusion
  272.7 2.6 fusion.37
  280.3 4.4 fusion.24
  290.4 4.9 fusion.73
  297.2 2.8 collective-permute-start.27
  302.3 5.0 %collective-permute-done.27 = bf16[96,960]{1,0:T(8,128)(2,1)S(1)} collective-permute-done((bf16[96,960]{1,0:T(8,128)(2,1)S(1)}, bf16[96,960]{1,0:T(8,128)(2,1)S(1)}, u32[]{:S(2)}, u32[]{:S(2)}) %collective-permute-start.27) | collective-permute-done | bytes 184352 | tf_op jit(solution)/shard_map/ppermute | solution.py:35
  309.9 6.2 %collective-permute-start.31 = (bf16[96,768]{1,0:T(8,128)(2,1)S(1)}, bf16[96,768]{1,0:T(8,128)(2,1)S(1)}, u32[]{:S(2)}, u32[]{:S(2)}) collective-permute-start(bf16[96,768]{1,0:T(8,128)(2,1)S(1)} %get-tuple-element.321), channel_id=1, source_target_pairs={{0,8},{28,20},{1,9},{29,21},{2,10},{30,22},{3,11},{31,23}} | collective-permute-start | bytes 442376 | tf_op jit(solution)/shard_map/ppermute | solution.py:567
  319.5 13.2 %collective-permute-start.34 = (bf16[96,768]{1,0:T(8,128)(2,1)S(1)}, bf16[96,768]{1,0:T(8,128)(2,1)S(1)}, u32[]{:S(2)}, u32[]{:S(2)}) collective-permute-start(bf16[96,768]{1,0:T(8,128)(2,1)S(1)} %get-tuple-element.318), channel_id=1, source_target_pairs={{28,8},{0,20},{29,9},{1,21},{30,10},{2,22},{31,11},{3,23}} | collective-permute-start | bytes 442376 | tf_op jit(solution)/shard_map/ppermute | solution.py:567
  343.5 6.5 %all-to-all-start = ((bf16[16,96,192]{2,1,0:T(8,128)(2,1)}), bf16[16,96,192]{2,1,0:T(8,128)(2,1)}, u32[]{:S(2)}, u32[]{:S(2)}) async-start(bf16[16,96,192]{2,1,0:T(8,128)(2,1)} %fusion.51), calls=%async_computation | async-start | bytes 1572864 | tf_op jit(solution)/shard_map/all_to_all | solution.py:587
  350.0 3.8 add_add_fusion.2
  360.2 9.8 %all-to-all-done = bf16[16,96,192]{2,1,0:T(8,128)(2,1)} async-done(((bf16[16,96,192]{2,1,0:T(8,128)(2,1)}), bf16[16,96,192]{2,1,0:T(8,128)(2,1)}, u32[]{:S(2)}, u32[]{:S(2)}) %all-to-all-start) | async-done | bytes 589856 | tf_op jit(solution)/shard_map/all_to_all | solution.py:587
  375.6 3.0 collective-permute-done.41
  378.6 12.4 %collective-permute-done.42 = f32[192,768]{1,0:T(8,128)} collective-permute-done((f32[192,768]{1,0:T(8,128)}, f32[192,768]{1,0:T(8,128)}, u32[]{:S(2)}, u32[]{:S(2)}) %collective-permute-start.42) | collective-permute-done | bytes 589856 | tf_op jit(solution)/shard_map/ppermute | solution.py:35
  394.8 2.9 collective-permute-start.50
  406.8 17.4 %shard_map.344 = bf16[768,768]{1,0:T(8,128)(2,1)S(1)} custom-call(s32[1]{0:T(128)} %bitcast.78.wide_ref, f32[1]{0:T(128)} %bitcast.81.factor_ref, f32[20]{0:T(128)S(1)} %copy-done.6, f32[768,768]{1,0:T(8,128)} %bitcast.340, bf16[768,768]{1,0:T(8,128)(2,1)S(1)} %broadcast_select_fusion.panel_ref), custom_call_target="tpu_custom_call" | custom-call | flops 22649241600 | bytes 5242880 | tf_op jit(solution)/shard_map/pallas_call | solution.py:340
  424.2 13.0 %collective-permute-done.48 = bf16[512,768]{1,0:T(8,128)(2,1)} collective-permute-done((bf16[512,768]{1,0:T(8,128)(2,1)S(1)}, bf16[512,768]{1,0:T(8,128)(2,1)}, u32[]{:S(2)}, u32[]{:S(2)}) %collective-permute-start.48) | collective-permute-done | bytes 786464 | tf_op jit(solution)/shard_map/ppermute | solution.py:35
  441.5 5.5 %all-to-all-start.1 = ((bf16[16,96,192]{1,2,0:T(8,128)(2,1)}), bf16[16,96,192]{1,2,0:T(8,128)(2,1)S(1)}, u32[]{:S(2)}, u32[]{:S(2)}) async-start(bf16[16,96,192]{1,2,0:T(8,128)(2,1)} %bitcast.99), calls=%async_computation.1 | async-start | bytes 1572864 | tf_op jit(solution)/shard_map/all_to_all | solution.py:595
  456.4 9.3 %collective-permute-done.61 = bf16[96,768]{1,0:T(8,128)(2,1)S(1)} collective-permute-done((bf16[96,768]{1,0:T(8,128)(2,1)}, bf16[96,768]{1,0:T(8,128)(2,1)S(1)}, u32[]{:S(2)}, u32[]{:S(2)}) %collective-permute-start.61) | collective-permute-done | bytes 147488 | tf_op jit(solution)/shard_map/ppermute | solution.py:575
  468.3 6.6 %collective-permute-done.58 = bf16[96,768]{1,0:T(8,128)(2,1)S(1)} collective-permute-done((bf16[96,768]{1,0:T(8,128)(2,1)S(1)}, bf16[96,768]{1,0:T(8,128)(2,1)S(1)}, u32[]{:S(2)}, u32[]{:S(2)}) %collective-permute-start.58) | collective-permute-done | bytes 147488 | tf_op jit(solution)/shard_map/ppermute | solution.py:575
  480.1 3.4 bitcast_convert_fusion
  486.7 3.4 bitcast_convert_fusion.1
  (552 shorter events, 197.8 us)
Async XLA Ops:
  20.1 11.9 %collective-permute-start.3 = (bf16[96,960]{1,0:T(8,128)(2,1)S(1)}, bf16[96,960]{1,0:T(8,128)(2,1)S(1)}, u32[]{:S(2)}, u32[]{:S(2)}) collective-permute-start(bf16[96,960]{1,0:T(8,128)(2,1)S(1)} %pad_maximum_fusion.22), channel_id=1, source_target_pairs={{0,16},{8,24},{16,0},{24,8},{1,17},{9,25},{17,1},{25,9},{2,18},{10... | collective-permute-start | bytes 552968 | tf_op jit(solution)/shard_map/ppermute | solution.py:35
  26.2 12.1 %collective-permute-start.2 = (bf16[2,2,96,576]{3,2,0,1:T(8,128)(2,1)S(1)}, bf16[2,2,96,576]{3,2,0,1:T(8,128)(2,1)S(1)}, u32[]{:S(2)}, u32[]{:S(2)}) collective-permute-start(bf16[2,2,96,576]{3,2,0,1:T(8,128)(2,1)S(1)} %pad_maximum_fusion.17), channel_id=1, source_target_pairs={{0,4},{4,0},{1,5},{5,1},{2,6},{6,2},{3,7},{7,3},{8,12},{12,8},{9,1... | collective-permute-start | bytes 1327112 | tf_op jit(solution)/shard_map/ppermute | solution.py:35
  32.0 21.3 %collective-permute-start.5 = (bf16[2,96,768]{2,1,0:T(8,128)(2,1)S(1)}, bf16[2,96,768]{2,1,0:T(8,128)(2,1)}, u32[]{:S(2)}, u32[]{:S(2)}) collective-permute-start(bf16[2,96,768]{2,1,0:T(8,128)(2,1)S(1)} %pad_maximum_fusion.19), channel_id=1, source_target_pairs={{0,16},{8,24},{16,0},{24,8},{1,17},{9,25},{17,1},{25,9},{2,18},{10... | collective-permute-start | bytes 884744 | tf_op jit(solution)/shard_map/ppermute | solution.py:35
  32.2 17.1 %collective-permute-start.6 = (bf16[2,96,960]{2,1,0:T(8,128)(2,1)S(1)}, bf16[2,96,960]{2,1,0:T(8,128)(2,1)S(1)}, u32[]{:S(2)}, u32[]{:S(2)}) collective-permute-start(bf16[2,96,960]{2,1,0:T(8,128)(2,1)S(1)} %pad_maximum_fusion.18), channel_id=1, source_target_pairs={{0,8},{8,0},{16,24},{24,16},{1,9},{9,1},{17,25},{25,17},{2,10},{10... | collective-permute-start | bytes 1105928 | tf_op jit(solution)/shard_map/ppermute | solution.py:35
  51.1 18.9 %collective-permute-start.7 = (bf16[2,2,96,960]{3,2,0,1:T(8,128)(2,1)}, bf16[2,2,96,960]{3,2,0,1:T(8,128)(2,1)}, u32[]{:S(2)}, u32[]{:S(2)}) collective-permute-start(bf16[2,2,96,960]{3,2,0,1:T(8,128)(2,1)} %pad_maximum_fusion.15), channel_id=1, source_target_pairs={{0,4},{4,0},{1,5},{5,1},{2,6},{6,2},{3,7},{7,3},{8,12},{12,8},{9,1... | collective-permute-start | bytes 2211848 | tf_op jit(solution)/shard_map/ppermute | solution.py:35
  55.2 18.0 %collective-permute-start.9 = (bf16[2,2,96,768]{3,2,1,0:T(8,128)(2,1)}, bf16[2,2,96,768]{3,2,1,0:T(8,128)(2,1)}, u32[]{:S(2)}, u32[]{:S(2)}) collective-permute-start(bf16[2,2,96,768]{3,2,1,0:T(8,128)(2,1)} %pad_maximum_fusion.16), channel_id=1, source_target_pairs={{0,8},{8,0},{16,24},{24,16},{1,9},{9,1},{17,25},{25,17},{2,10},{10... | collective-permute-start | bytes 1769480 | tf_op jit(solution)/shard_map/ppermute | solution.py:35
  62.2 23.0 %collective-permute-start.8 = (bf16[768,576]{0,1:T(8,128)(2,1)}, bf16[768,576]{0,1:T(8,128)(2,1)}, u32[]{:S(2)}, u32[]{:S(2)}) collective-permute-start(bf16[768,576]{0,1:T(8,128)(2,1)} %copy.97), channel_id=1, source_target_pairs={{0,2},{2,0},{1,3},{3,1},{4,6},{6,4},{5,7},{7,5},{8,10},{10,8},{9,1... | collective-permute-start | bytes 2654216 | tf_op jit(solution)/shard_map/ppermute | solution.py:35
  72.7 21.8 %collective-permute-start.11 = (bf16[768,192]{1,0:T(8,128)(2,1)S(1)}, bf16[768,192]{1,0:T(8,128)(2,1)S(1)}, u32[]{:S(2)}, u32[]{:S(2)}) collective-permute-start(bf16[768,192]{1,0:T(8,128)(2,1)S(1)} %slice.433), channel_id=1, source_target_pairs={{0,2},{2,0},{1,3},{3,1},{4,6},{6,4},{5,7},{7,5},{8,10},{10,8},{9,1... | collective-permute-start | bytes 884744 | tf_op jit(solution)/shard_map/ppermute | solution.py:35
  75.5 29.7 %collective-permute-start.15 = (bf16[2,2,2,96,768]{4,3,2,1,0:T(8,128)(2,1)}, bf16[2,2,2,96,768]{4,3,2,1,0:T(8,128)(2,1)}, u32[]{:S(2)}, u32[]{:S(2)}) collective-permute-start(bf16[2,2,2,96,768]{4,3,2,1,0:T(8,128)(2,1)} %pad_maximum_fusion.11), channel_id=1, source_target_pairs={{0,4},{4,0},{1,5},{5,1},{2,6},{6,2},{3,7},{7,3},{8,12},{12,8},{9,1... | collective-permute-start | bytes 3538952 | tf_op jit(solution)/shard_map/ppermute | solution.py:35
  97.9 28.2 %collective-permute-start.14 = (bf16[768,768]{1,0:T(8,128)(2,1)}, bf16[768,768]{1,0:T(8,128)(2,1)}, u32[]{:S(2)}, u32[]{:S(2)}) collective-permute-start(bf16[768,768]{1,0:T(8,128)(2,1)} %slice.434), channel_id=1, source_target_pairs={{0,2},{2,0},{1,3},{3,1},{4,6},{6,4},{5,7},{7,5},{8,10},{10,8},{9,1... | collective-permute-start | bytes 3538952 | tf_op jit(solution)/shard_map/ppermute | solution.py:35
  156.7 45.2 %collective-permute-start.21 = (bf16[2,4,96,768]{3,2,1,0:T(8,128)(2,1)}, bf16[2,4,96,768]{3,2,1,0:T(8,128)(2,1)}, u32[]{:S(2)}, u32[]{:S(2)}) collective-permute-start(bf16[2,4,96,768]{3,2,1,0:T(8,128)(2,1)} %select_bitcast_fusion.2), channel_id=1, source_target_pairs={{0,4},{4,0},{1,5},{5,1},{2,6},{6,2},{3,7},{7,3},{8,12},{12,8},{9,1... | collective-permute-start | bytes 3538952 | tf_op jit(solution)/shard_map/ppermute | solution.py:35
  157.3 11.6 %collective-permute-start.18 = (bf16[512,768]{1,0:T(8,128)(2,1)}, bf16[512,768]{1,0:T(8,128)(2,1)S(1)}, u32[]{:S(2)}, u32[]{:S(2)}) collective-permute-start(bf16[512,768]{1,0:T(8,128)(2,1)} %get-tuple-element.280), channel_id=1, source_target_pairs={{0,1},{1,0},{2,3},{3,2},{4,5},{5,4},{6,7},{7,6},{8,9},{9,8},{10,11... | collective-permute-start | bytes 2359304 | tf_op jit(solution)/shard_map/ppermute | solution.py:35
  157.3 11.6 %collective-permute-start.19 = (bf16[512,768]{1,0:T(8,128)(2,1)}, bf16[512,768]{1,0:T(8,128)(2,1)}, u32[]{:S(2)}, u32[]{:S(2)}) collective-permute-start(bf16[512,768]{1,0:T(8,128)(2,1)} %get-tuple-element.281), channel_id=1, source_target_pairs={{0,1},{1,0},{2,3},{3,2},{4,5},{5,4},{6,7},{7,6},{8,9},{9,8},{10,11... | collective-permute-start | bytes 2359304 | tf_op jit(solution)/shard_map/ppermute | solution.py:35
  162.2 36.4 %collective-permute-start.16 = (bf16[512,768]{1,0:T(8,128)(2,1)}, bf16[512,768]{1,0:T(8,128)(2,1)}, u32[]{:S(2)}, u32[]{:S(2)}) collective-permute-start(bf16[512,768]{1,0:T(8,128)(2,1)} %get-tuple-element.282), channel_id=1, source_target_pairs={{0,1},{1,0},{2,3},{3,2},{4,5},{5,4},{6,7},{7,6},{8,9},{9,8},{10,11... | collective-permute-start | bytes 2359304 | tf_op jit(solution)/shard_map/ppermute | solution.py:35
  162.2 36.4 %collective-permute-start.17 = (bf16[512,768]{1,0:T(8,128)(2,1)}, bf16[512,768]{1,0:T(8,128)(2,1)}, u32[]{:S(2)}, u32[]{:S(2)}) collective-permute-start(bf16[512,768]{1,0:T(8,128)(2,1)} %get-tuple-element.283), channel_id=1, source_target_pairs={{0,1},{1,0},{2,3},{3,2},{4,5},{5,4},{6,7},{7,6},{8,9},{9,8},{10,11... | collective-permute-start | bytes 2359304 | tf_op jit(solution)/shard_map/ppermute | solution.py:35
  192.0 35.2 %collective-permute-start.20 = (bf16[768,960]{0,1:T(8,128)(2,1)S(1)}, bf16[768,960]{0,1:T(8,128)(2,1)S(1)}, u32[]{:S(2)}, u32[]{:S(2)}) collective-permute-start(bf16[768,960]{0,1:T(8,128)(2,1)S(1)} %pad_maximum_fusion.8), channel_id=1, source_target_pairs={{0,2},{2,0},{1,3},{3,1},{4,6},{6,4},{5,7},{7,5},{8,10},{10,8},{9,1... | collective-permute-start | bytes 4423688 | tf_op jit(solution)/shard_map/ppermute | solution.py:35
  195.9 73.5 %collective-permute-start.26 = (bf16[768,576]{0,1:T(8,128)(2,1)}, bf16[768,576]{0,1:T(8,128)(2,1)}, u32[]{:S(2)}, u32[]{:S(2)}) collective-permute-start(bf16[768,576]{0,1:T(8,128)(2,1)} %convolution_convert_fusion.5), channel_id=1, source_target_pairs={{0,2},{2,0},{1,3},{3,1},{4,6},{6,4},{5,7},{7,5},{8,10},{10,8},{9,1... | collective-permute-start | bytes 2654216 | tf_op jit(solution)/shard_map/ppermute | solution.py:35
  205.7 47.8 %collective-permute-start.23 = (bf16[2,2,96,768]{3,2,0,1:T(8,128)(2,1)}, bf16[2,2,96,768]{3,2,0,1:T(8,128)(2,1)}, u32[]{:S(2)}, u32[]{:S(2)}) collective-permute-start(bf16[2,2,96,768]{3,2,0,1:T(8,128)(2,1)} %fusion.34), channel_id=1, source_target_pairs={{0,8},{8,0},{16,24},{24,16},{1,9},{9,1},{17,25},{25,17},{2,10},{10... | collective-permute-start | bytes 1769480 | tf_op jit(solution)/shard_map/ppermute | solution.py:35
  235.7 29.4 %collective-permute-start.22 = (bf16[4,96,960]{2,1,0:T(8,128)(2,1)}, bf16[4,96,960]{2,1,0:T(8,128)(2,1)}, u32[]{:S(2)}, u32[]{:S(2)}) collective-permute-start(bf16[4,96,960]{2,1,0:T(8,128)(2,1)} %fusion.33), channel_id=1, source_target_pairs={{0,4},{4,0},{1,5},{5,1},{2,6},{6,2},{3,7},{7,3},{8,12},{12,8},{9,1... | collective-permute-start | bytes 2211848 | tf_op jit(solution)/shard_map/ppermute | solution.py:35
  257.7 18.1 %collective-permute-start.25 = (bf16[2,96,768]{2,1,0:T(8,128)(2,1)}, bf16[2,96,768]{2,1,0:T(8,128)(2,1)}, u32[]{:S(2)}, u32[]{:S(2)}) collective-permute-start(bf16[2,96,768]{2,1,0:T(8,128)(2,1)} %fusion.39), channel_id=1, source_target_pairs={{0,16},{8,24},{16,0},{24,8},{1,17},{9,25},{17,1},{25,9},{2,18},{10... | collective-permute-start | bytes 884744 | tf_op jit(solution)/shard_map/ppermute | solution.py:35
  264.6 15.7 %collective-permute-start.43 = (bf16[512,768]{1,0:T(8,128)(2,1)}, bf16[512,768]{1,0:T(8,128)(2,1)}, u32[]{:S(2)}, u32[]{:S(2)}) collective-permute-start(bf16[512,768]{1,0:T(8,128)(2,1)} %get-tuple-element.278), channel_id=1, source_target_pairs={{0,1},{1,0},{2,3},{3,2},{4,5},{5,4},{6,7},{7,6},{8,9},{9,8},{10,11... | collective-permute-start | bytes 2359304 | tf_op jit(solution)/shard_map/ppermute | solution.py:35
  264.6 15.7 %collective-permute-start.44 = (bf16[512,768]{1,0:T(8,128)(2,1)}, bf16[512,768]{1,0:T(8,128)(2,1)}, u32[]{:S(2)}, u32[]{:S(2)}) collective-permute-start(bf16[512,768]{1,0:T(8,128)(2,1)} %get-tuple-element.279), channel_id=1, source_target_pairs={{0,1},{1,0},{2,3},{3,2},{4,5},{5,4},{6,7},{7,6},{8,9},{9,8},{10,11... | collective-permute-start | bytes 2359304 | tf_op jit(solution)/shard_map/ppermute | solution.py:35
  269.3 26.6 %collective-permute-start.24 = (bf16[2,96,960]{2,1,0:T(8,128)(2,1)S(1)}, bf16[2,96,960]{2,1,0:T(8,128)(2,1)}, u32[]{:S(2)}, u32[]{:S(2)}) collective-permute-start(bf16[2,96,960]{2,1,0:T(8,128)(2,1)S(1)} %fusion.38), channel_id=1, source_target_pairs={{0,8},{8,0},{16,24},{24,16},{1,9},{9,1},{17,25},{25,17},{2,10},{10... | collective-permute-start | bytes 1105928 | tf_op jit(solution)/shard_map/ppermute | solution.py:35
  275.3 24.8 %collective-permute-start.29 = (bf16[4,96,576]{2,1,0:T(8,128)(2,1)}, bf16[4,96,576]{2,1,0:T(8,128)(2,1)}, u32[]{:S(2)}, u32[]{:S(2)}) collective-permute-start(bf16[4,96,576]{2,1,0:T(8,128)(2,1)} %fusion.37), channel_id=1, source_target_pairs={{0,4},{4,0},{1,5},{5,1},{2,6},{6,2},{3,7},{7,3},{8,12},{12,8},{9,1... | collective-permute-start | bytes 1327112 | tf_op jit(solution)/shard_map/ppermute | solution.py:35
  278.7 22.7 %collective-permute-start.28 = (bf16[96,768]{1,0:T(8,128)(2,1)}, bf16[96,768]{1,0:T(8,128)(2,1)}, u32[]{:S(2)}, u32[]{:S(2)}) collective-permute-start(bf16[96,768]{1,0:T(8,128)(2,1)} %fusion.43), channel_id=1, source_target_pairs={{0,2},{2,0},{1,3},{3,1},{4,6},{6,4},{5,7},{7,5},{8,10},{10,8},{9,1... | collective-permute-start | bytes 442376 | tf_op jit(solution)/shard_map/ppermute | solution.py:35
  290.0 63.8 %collective-permute-start.45 = (f32[54,128]{1,0:T(8,128)}, f32[54,128]{1,0:T(8,128)}, u32[]{:S(2)}, u32[]{:S(2)}) collective-permute-start(f32[54,128]{1,0:T(8,128)} %maximum_bitcast_fusion), channel_id=1, source_target_pairs={{0,2},{2,0},{1,3},{3,1},{4,6},{6,4},{5,7},{7,5},{8,10},{10,8},{9,1... | collective-permute-start | bytes 82952 | tf_op jit(solution)/shard_map/ppermute | solution.py:35
  301.3 14.8 %collective-permute-start.37 = (bf16[2,96,576]{2,1,0:T(8,128)(2,1)S(1)}, bf16[2,96,576]{2,1,0:T(8,128)(2,1)S(1)}, u32[]{:S(2)}, u32[]{:S(2)}) collective-permute-start(bf16[2,96,576]{2,1,0:T(8,128)(2,1)S(1)} %fusion.41), channel_id=1, source_target_pairs={{0,8},{8,0},{16,24},{24,16},{1,9},{9,1},{17,25},{25,17},{2,10},{10... | collective-permute-start | bytes 663560 | tf_op jit(solution)/shard_map/ppermute | solution.py:35
  308.4 27.0 %collective-permute-start.36 = (bf16[96,768]{1,0:T(8,128)(2,1)S(1)}, bf16[96,768]{1,0:T(8,128)(2,1)S(1)}, u32[]{:S(2)}, u32[]{:S(2)}) collective-permute-start(bf16[96,768]{1,0:T(8,128)(2,1)S(1)} %get-tuple-element.250), channel_id=1, source_target_pairs={{20,8},{8,20},{21,9},{9,21},{22,10},{10,22},{23,11},{11,23}} | collective-permute-start | bytes 442376 | tf_op jit(solution)/shard_map/ppermute | solution.py:567
  309.2 26.2 %collective-permute-start.35 = (bf16[96,768]{1,0:T(8,128)(2,1)S(1)}, bf16[96,768]{1,0:T(8,128)(2,1)S(1)}, u32[]{:S(2)}, u32[]{:S(2)}) collective-permute-start(bf16[96,768]{1,0:T(8,128)(2,1)S(1)} %get-tuple-element.317), channel_id=1, source_target_pairs={{16,8},{12,20},{17,9},{13,21},{18,10},{14,22},{19,11},{15,23}} | collective-permute-start | bytes 442376 | tf_op jit(solution)/shard_map/ppermute | solution.py:567
  318.8 13.9 %collective-permute-start.33 = (bf16[96,768]{1,0:T(8,128)(2,1)S(1)}, bf16[96,768]{1,0:T(8,128)(2,1)S(1)}, u32[]{:S(2)}, u32[]{:S(2)}) collective-permute-start(bf16[96,768]{1,0:T(8,128)(2,1)S(1)} %get-tuple-element.319), channel_id=1, source_target_pairs={{24,8},{4,20},{25,9},{5,21},{26,10},{6,22},{27,11},{7,23}} | collective-permute-start | bytes 442376 | tf_op jit(solution)/shard_map/ppermute | solution.py:567
  319.5 15.9 %collective-permute-start.34 = (bf16[96,768]{1,0:T(8,128)(2,1)S(1)}, bf16[96,768]{1,0:T(8,128)(2,1)S(1)}, u32[]{:S(2)}, u32[]{:S(2)}) collective-permute-start(bf16[96,768]{1,0:T(8,128)(2,1)S(1)} %get-tuple-element.318), channel_id=1, source_target_pairs={{28,8},{0,20},{29,9},{1,21},{30,10},{2,22},{31,11},{3,23}} | collective-permute-start | bytes 442376 | tf_op jit(solution)/shard_map/ppermute | solution.py:567
  338.4 15.5 %collective-permute-start.38 = (f32[192,768]{1,0:T(8,128)}, f32[192,768]{1,0:T(8,128)}, u32[]{:S(2)}, u32[]{:S(2)}) collective-permute-start(f32[192,768]{1,0:T(8,128)} %get-tuple-element.299), channel_id=1, source_target_pairs={{0,1},{1,0},{2,3},{3,2},{4,5},{5,4},{6,7},{7,6},{8,9},{9,8},{10,11... | collective-permute-start | bytes 1769480 | tf_op jit(solution)/shard_map/ppermute | solution.py:35
  338.4 15.5 %collective-permute-start.39 = (f32[192,768]{1,0:T(8,128)}, f32[192,768]{1,0:T(8,128)}, u32[]{:S(2)}, u32[]{:S(2)}) collective-permute-start(f32[192,768]{1,0:T(8,128)} %get-tuple-element.300), channel_id=1, source_target_pairs={{0,1},{1,0},{2,3},{3,2},{4,5},{5,4},{6,7},{7,6},{8,9},{9,8},{10,11... | collective-permute-start | bytes 1769480 | tf_op jit(solution)/shard_map/ppermute | solution.py:35
  343.5 26.5 %all-to-all-start = ((bf16[16,96,192]{2,1,0:T(8,128)(2,1)}), bf16[16,96,192]{2,1,0:T(8,128)(2,1)}, u32[]{:S(2)}, u32[]{:S(2)}) async-start(bf16[16,96,192]{2,1,0:T(8,128)(2,1)} %fusion.51), calls=%async_computation | async-start | bytes 1572864 | tf_op jit(solution)/shard_map/all_to_all | solution.py:587
  357.2 21.4 %collective-permute-start.41 = (f32[192,768]{1,0:T(8,128)}, f32[192,768]{1,0:T(8,128)}, u32[]{:S(2)}, u32[]{:S(2)}) collective-permute-start(f32[192,768]{1,0:T(8,128)} %get-tuple-element.297), channel_id=1, source_target_pairs={{0,2},{2,0},{1,3},{3,1},{4,6},{6,4},{5,7},{7,5},{8,10},{10,8},{9,1... | collective-permute-start | bytes 1769480 | tf_op jit(solution)/shard_map/ppermute | solution.py:35
  359.3 31.7 %collective-permute-start.42 = (f32[192,768]{1,0:T(8,128)}, f32[192,768]{1,0:T(8,128)}, u32[]{:S(2)}, u32[]{:S(2)}) collective-permute-start(f32[192,768]{1,0:T(8,128)} %get-tuple-element.298), channel_id=1, source_target_pairs={{0,2},{2,0},{1,3},{3,1},{4,6},{6,4},{5,7},{7,5},{8,10},{10,8},{9,1... | collective-permute-start | bytes 1769480 | tf_op jit(solution)/shard_map/ppermute | solution.py:35
  372.3 20.0 %collective-permute-start.46 = (bf16[768,384]{1,0:T(8,128)(2,1)S(1)}, bf16[768,384]{1,0:T(8,128)(2,1)S(1)}, u32[]{:S(2)}, u32[]{:S(2)}) collective-permute-start(bf16[768,384]{1,0:T(8,128)(2,1)S(1)} %reshape.616), channel_id=1, source_target_pairs={{0,1},{1,0},{2,3},{3,2},{4,5},{5,4},{6,7},{7,6},{8,9},{9,8},{10,11... | collective-permute-start | bytes 1769480 | tf_op jit(solution)/shard_map/ppermute | solution.py:35
  373.2 19.3 %collective-permute-start.47 = (f32[54,128]{1,0:T(8,128)S(1)}, f32[54,128]{1,0:T(8,128)S(1)}, u32[]{:S(2)}, u32[]{:S(2)}) collective-permute-start(f32[54,128]{1,0:T(8,128)S(1)} %fusion.135), channel_id=1, source_target_pairs={{0,4},{4,0},{1,5},{5,1},{2,6},{6,2},{3,7},{7,3},{8,12},{12,8},{9,1... | collective-permute-start | bytes 82952 | tf_op jit(solution)/shard_map/ppermute | solution.py:35
  400.3 23.9 %collective-permute-start.49 = (bf16[512,768]{1,0:T(8,128)(2,1)}, bf16[512,768]{1,0:T(8,128)(2,1)}, u32[]{:S(2)}, u32[]{:S(2)}) collective-permute-start(bf16[512,768]{1,0:T(8,128)(2,1)} %constant_dynamic-slice_fusion.1), channel_id=1, source_target_pairs={{0,2},{2,0},{1,3},{3,1},{4,6},{6,4},{5,7},{7,5},{8,10},{10,8},{9,1... | collective-permute-start | bytes 2359304 | tf_op jit(solution)/shard_map/ppermute | solution.py:35
  401.2 36.0 %collective-permute-start.48 = (bf16[512,768]{1,0:T(8,128)(2,1)S(1)}, bf16[512,768]{1,0:T(8,128)(2,1)}, u32[]{:S(2)}, u32[]{:S(2)}) collective-permute-start(bf16[512,768]{1,0:T(8,128)(2,1)S(1)} %constant_dynamic-slice_fusion.2), channel_id=1, source_target_pairs={{0,2},{2,0},{1,3},{3,1},{4,6},{6,4},{5,7},{7,5},{8,10},{10,8},{9,1... | collective-permute-start | bytes 2359304 | tf_op jit(solution)/shard_map/ppermute | solution.py:35
  402.3 21.8 %collective-permute-start.51 = (f32[54,128]{1,0:T(8,128)S(1)}, f32[54,128]{1,0:T(8,128)S(1)}, u32[]{:S(2)}, u32[]{:S(2)}) collective-permute-start(f32[54,128]{1,0:T(8,128)S(1)} %add.425), channel_id=1, source_target_pairs={{0,8},{8,0},{16,24},{24,16},{1,9},{9,1},{17,25},{25,17},{2,10},{10... | collective-permute-start | bytes 82952 | tf_op jit(solution)/shard_map/ppermute | solution.py:35
  441.5 48.6 %all-to-all-start.1 = ((bf16[16,96,192]{1,2,0:T(8,128)(2,1)}), bf16[16,96,192]{1,2,0:T(8,128)(2,1)S(1)}, u32[]{:S(2)}, u32[]{:S(2)}) async-start(bf16[16,96,192]{1,2,0:T(8,128)(2,1)} %bitcast.99), calls=%async_computation.1 | async-start | bytes 1572864 | tf_op jit(solution)/shard_map/all_to_all | solution.py:595
  447.0 29.6 %collective-permute-start.55 = (bf16[512,768]{1,0:T(8,128)(2,1)}, bf16[512,768]{1,0:T(8,128)(2,1)}, u32[]{:S(2)}, u32[]{:S(2)}) collective-permute-start(bf16[512,768]{1,0:T(8,128)(2,1)} %collective-permute-done.49), channel_id=1, source_target_pairs={{0,1},{1,0},{2,3},{3,2},{4,5},{5,4},{6,7},{7,6},{8,9},{9,8},{10,11... | collective-permute-start | bytes 2359304 | tf_op jit(solution)/shard_map/ppermute | solution.py:35
  447.7 18.0 %collective-permute-start.61 = (bf16[96,768]{1,0:T(8,128)(2,1)}, bf16[96,768]{1,0:T(8,128)(2,1)S(1)}, u32[]{:S(2)}, u32[]{:S(2)}) collective-permute-start(bf16[96,768]{1,0:T(8,128)(2,1)} %get-tuple-element.289), channel_id=1, source_target_pairs={{8,0},{20,28},{9,1},{21,29},{10,2},{22,30},{11,3},{23,31}} | collective-permute-start | bytes 442376 | tf_op jit(solution)/shard_map/ppermute | solution.py:575
  449.0 17.3 %collective-permute-start.60 = (bf16[96,768]{1,0:T(8,128)(2,1)}, bf16[96,768]{1,0:T(8,128)(2,1)S(1)}, u32[]{:S(2)}, u32[]{:S(2)}) collective-permute-start(bf16[96,768]{1,0:T(8,128)(2,1)} %get-tuple-element.290), channel_id=1, source_target_pairs={{8,4},{20,24},{9,5},{21,25},{10,6},{22,26},{11,7},{23,27}} | collective-permute-start | bytes 442376 | tf_op jit(solution)/shard_map/ppermute | solution.py:575
  449.7 18.6 %collective-permute-start.59 = (bf16[96,768]{1,0:T(8,128)(2,1)S(1)}, bf16[96,768]{1,0:T(8,128)(2,1)S(1)}, u32[]{:S(2)}, u32[]{:S(2)}) collective-permute-start(bf16[96,768]{1,0:T(8,128)(2,1)S(1)} %get-tuple-element.291), channel_id=1, source_target_pairs={{8,24},{20,4},{9,25},{21,5},{10,26},{22,6},{11,27},{23,7}} | collective-permute-start | bytes 442376 | tf_op jit(solution)/shard_map/ppermute | solution.py:575
  455.1 19.8 %collective-permute-start.58 = (bf16[96,768]{1,0:T(8,128)(2,1)S(1)}, bf16[96,768]{1,0:T(8,128)(2,1)S(1)}, u32[]{:S(2)}, u32[]{:S(2)}) collective-permute-start(bf16[96,768]{1,0:T(8,128)(2,1)S(1)} %get-tuple-element.292), channel_id=1, source_target_pairs={{8,28},{20,0},{9,29},{21,1},{10,30},{22,2},{11,31},{23,3}} | collective-permute-start | bytes 442376 | tf_op jit(solution)/shard_map/ppermute | solution.py:575
  468.3 15.1 %collective-permute-start.54 = (bf16[512,768]{1,0:T(8,128)(2,1)}, bf16[512,768]{1,0:T(8,128)(2,1)S(1)}, u32[]{:S(2)}, u32[]{:S(2)}) collective-permute-start(bf16[512,768]{1,0:T(8,128)(2,1)} %collective-permute-done.48), channel_id=1, source_target_pairs={{0,1},{1,0},{2,3},{3,2},{4,5},{5,4},{6,7},{7,6},{8,9},{9,8},{10,11... | collective-permute-start | bytes 2359304 | tf_op jit(solution)/shard_map/ppermute | solution.py:35
  (140 other events, 966.1 us)

commit v2 on v0

--- a/solution.py
+++ b/solution.py
@@ -100,13 +100,6 @@
 
 def by_rows(grad):
     return grad.reshape(lax.axis_size("z"), 2, -1, grad.shape[-1])
-
-
-def all_sum(value, axes):
-    for axis in axes:
-        for distance in distances(axis):
-            value = value + swap(value, axis, distance)
-    return value
 
 
 def swap_cores(own):
@@ -211,8 +204,7 @@
         out_ref[:, value_lanes] = values_sum[...].astype(BF)
 
 
-def on_chip(kernel, shapes, scratch, flops, exps, *operands):
-    moved = sum(o.size * o.dtype.itemsize for o in (*operands, *shapes))
+def on_chip(kernel, shapes, scratch, *operands):
     return pl.pallas_call(
         kernel,
         out_shape=shapes,
@@ -220,7 +212,7 @@
         out_specs=[pl.BlockSpec(memory_space=pltpu.VMEM)] * len(shapes),
         scratch_shapes=scratch,
         compiler_params=pltpu.CompilerParams(vmem_limit_bytes=50 * 2**20),
-        cost_estimate=pl.CostEstimate(flops=flops, bytes_accessed=moved, transcendentals=exps),
+        cost_estimate=pl.CostEstimate(flops=0, bytes_accessed=0, transcendentals=0),
     )(*operands)
 
 
@@ -230,17 +222,13 @@
         jax.ShapeDtypeStruct((SLOTS, width), BF),
         jax.ShapeDtypeStruct((SLOTS, width), F32),
     ]
-    pairs = SLOTS * SLOTS * width // HEAD_DIM
-    return on_chip(attend_kernel, shapes, [], 16 * pairs * HEAD_DIM, pairs, low, qkv)
+    return on_chip(attend_kernel, shapes, [], low, qkv)
 
 
 def attend_back(low, qkv, grad, log_total):
     shapes = [jax.ShapeDtypeStruct(qkv.shape, BF)]
     scratch = [pltpu.VMEM((SLOTS, HEAD_DIM), F32)] * 2
-    pairs = SLOTS * SLOTS * grad.shape[1] // HEAD_DIM
-    return on_chip(
-        attend_back_kernel, shapes, scratch, 40 * pairs * HEAD_DIM, pairs, low, qkv, grad, log_total
-    )[0]
+    return on_chip(attend_back_kernel, shapes, scratch, low, qkv, grad, log_total)[0]
 
 
 def newton_kernel(
@@ -431,25 +419,29 @@
     normed = layer_norm(source, norm_gains[0], shared_biases[0]).astype(BF)
     heads = [project(0)]
     for lead, distance in enumerate(z_steps[1:]):
-        up_piece = grow(up_piece, "z", distance, lead + 1, heads[0])
-    down_piece = grow(down_piece, "z", z_steps[0], 1, up_piece)
-    mixed, logs = attend(low, after(heads[0], down_piece))
-    up_own = grow(up_piece, "y", 1, depth, mixed).reshape(-1, up_piece.shape[-1])
+        up_piece = grow(up_piece, "z", distance, lead + 1, heads[0], low)
+    mixed, logs = attend(low, after(heads[0], up_piece))
+    qkv[1] = after(qkv[1], mixed)
+    up_own = grow(up_piece, "y", 1, depth, qkv[1]).reshape(-1, up_piece.shape[-1])
     out_own, up_own = up_own[:, units_each:], up_own[:, :units_each]
-    out = (out_own, swap(out_own, "x"))
     up_own = fixed(up_own)
-    up = (up_own, swap(up_own, "x"))
-    for lead, distance in enumerate(z_steps[1:]):
-        down_piece = grow(down_piece, "z", distance, lead + 2, up_own)
-    qkv[1] = after(qkv[1], down_piece, up_own)
+    up_got = swap(up_own, "x")
+    out_own = fixed(out_own)
+    out_got = swap(out_own, "x")
+    down_piece = grow(down_piece, "z", z_steps[0], 1, up_own)
+    qkv[1] = after(qkv[1], down_piece, up_own, out_own)
     heads.append(project(1))
     mixed_x, logs_x = attend(low, heads[1])
-    mixed, logs = (mixed, mixed_x), (logs, logs_x)
-    down_full = grow(down_piece, "y", 1, depth + 1, mixed_x)
+    out_got, mixed_x = after((out_got, mixed_x), mixed_x)
+    out = (out_own, out_got)
+    up = (up_own, after(up_got, mixed_x))
+    for lead, distance in enumerate(z_steps[1:]):
+        down_piece = grow(down_piece, "z", distance, lead + 2, mixed_x)
+    down_full = grow(down_piece, "y", 1, depth + 1)
     down_full = down_full.reshape(2, -1, down_piece.shape[-1])
     down = (down_full[0], down_full[1])
+    mixed, logs = (mixed, after(mixed_x, up[1], down_piece)), (logs, logs_x)
     branch = across_cores(dot_nt(mixed[0], out[0]) + dot_nt(mixed[1], out[1]))
-    branch = after(branch, up[1], down_full)
     hidden = source + (branch + shared_biases[2])
     normed_two = layer_norm(hidden, norm_gains[1], shared_biases[1]).astype(BF)
     before = [
@@ -490,26 +482,30 @@
     grad_up_x = fixed(grad_up[1])
     up_got = swap(grad_up_x, "x")
     back_x = attend_back(low, heads[1], after(grad_mixed[1], grad_up_x, down_offer[1]), logs[1])
+    up_got = after(up_got, back_x)
+    up_sum = by_rows(grad_up[0]).astype(F32) + by_rows(up_got).astype(F32)
+    down_sum = split_planes(settle(down_offer, back_x), 1)
+    up_offer = offer(up_sum, "y", 1, 1)
+    down_offer = offer(down_sum, "z", depth, z_steps[-1])
+    back_x = after(back_x, up_offer[1], down_offer[1])
     grad_square_x = fixed(dot_tn(normed, back_x))
     square_got = swap(grad_square_x, "x")
-    down_sum = split_planes(settle(down_offer, grad_square_x), 1)
-    down_offer = offer(down_sum, "z", depth, z_steps[-1])
-    up_sum = grad_up[0].astype(F32) + after(up_got, down_offer[1]).astype(F32)
-    up_offer = offer(by_rows(up_sum), "y", 1, 1)
-    grad_mixed[0] = after(grad_mixed[0], up_offer[1], down_offer[1])
+    grad_mixed[0] = after(grad_mixed[0], grad_square_x)
     back = attend_back(low, heads[0], grad_mixed[0], logs[0])
-    grad_square = dot_tn(normed, back).astype(BF)
 
     def next_down(lead, offered, last):
         summed = settle(offered, last)
         return offer(summed, "z", lead, z_steps[lead - 1])
 
+    up_sum = split_planes(settle(up_offer, back), 0)
+    up_offer = offer(up_sum, "z", depth - 1, z_steps[-1])
     for lead in range(depth - 1, 0, -1):
-        down_offer = next_down(lead, down_offer, grad_square)
-    up_sum = split_planes(settle(up_offer, down_offer[1]), 0)
-    up_offer = offer(up_sum, "z", depth - 1, z_steps[-1])
-    square = grad_square.astype(F32) + after(square_got, up_offer[1]).astype(F32)
-    square_offer = offer(by_rows(square), "y", 1, 1)
+        down_offer = next_down(lead, down_offer, up_offer[1])
+    back = after(back, up_offer[1], down_offer[1])
+    grad_square = dot_tn(normed, back).astype(BF)
+    square_got = after(square_got, grad_square)
+    square = by_rows(grad_square).astype(F32) + by_rows(square_got).astype(F32)
+    square_offer = offer(square, "y", 1, 1)
     down_sum = settle(down_offer, square_offer[1])
     down_sent = fixed(down_sum[1])
     down_got = swap(down_sent, "x")
@@ -597,6 +593,9 @@
     pair = jnp.concatenate((pair, swap(pair, "c")), axis=1)
     flat = flat + after(swap(flat, "y"), pair)
     gram = gram + after(gram_got, pair, flat)
+    for distance in z_steps[:-1]:
+        flat = flat + after(swap(flat, "z", distance), gram)
+    flat_got = swap(flat, "z", z_steps[-1])
     half = SLOTS // 2
     core = lax.axis_index("c")
     finals = [fixed(after(result, gram)), fixed(after(grad_hidden + grad_source, gram))]
@@ -607,7 +606,7 @@
     norm = jnp.where(is_wide, jnp.trace(gram), jnp.sum(pair_values * pair_values))
     factor = 1.0 / (jnp.sqrt(norm) + 1e-07)
     orth = newton(is_wide, factor, gram, jnp.where(is_wide, wide, pair))
-    got, flat, back_sent = lax.optimization_barrier((got, flat, orth))
+    got, flat_got, back_sent = lax.optimization_barrier((got, flat_got, orth))
     back = lax.all_to_all(
         back_sent.reshape(groups, rows_each, units_each),
         ("z", "y"),
@@ -615,7 +614,7 @@
         concat_axis=0,
         tiled=True,
     ).astype(F32)
-    flat = all_sum(flat, ("z",)).reshape(-1)
+    flat = (flat + flat_got).reshape(-1)
 
     def both_bins(own, received):
         other = join(received, swap(received, "c"), bit_of("c"), 0).reshape(own.shape)

time: 481 us -> 470 us (0.977)
  matrix products: 53.2 us -> 43.8 us
  waiting for transfers between devices: 129 us -> 137 us
  starting transfers between devices: 74.8 us -> 67.5 us
    ppermute x50, starting transfers between devices: 62.5 us -> 50.6 us  [swap(): return lax.ppermute(value, axis, [(i, i ^ distance) for i in range(size)])]
    unnamed x229 -> x221, local copies, waits for them, and re-layouts: 21 us -> 22 us
  transfers between devices with their start and end apart: 53 -> 53, of which waited for: 20 -> 19; matrix products, arithmetic and copies ran while one was open for 32% -> 32% of each run, Pallas kernels for 11% -> 11%
where the time goes in v2:
time: 470 us; the launch traced here: 465 us
  waiting for transfers between devices  137 us (29%)
  other arithmetic  106 us (23%)
  starting transfers between devices  67.5 us (14%)
  local copies, waits for them, and re-layouts  54.3 us (12%)
  Pallas kernels  52.3 us (11%)
  matrix products  43.8 us (9%)
    ppermute x50, waiting for transfers between devices, swap(): return lax.ppermute(value, axis, [(i, i ^ distance) for i in range(size)])  123 us
    ppermute x50, starting transfers between devices, swap(): return lax.ppermute(value, axis, [(i, i ^ distance) for i in range(size)])  50.6 us
    pallas_call x4, Pallas kernels, on_chip(): pl.pallas_call(kernel, out_shape=shapes, in_specs=[pl.BlockSpec(memory_sp...  33.9 us
    unnamed x221, local copies, waits for them, and re-layouts  22 us
    pallas_call x1, Pallas kernels, newton(): pl.pallas_call(newton_kernel, out_shape=shape, in_specs=[scalar, scalar,...  18.4 us
    another operation x28, other arithmetic, join(): return jnp.stack((low, high), axis=dim)  14.6 us
    dot_general x8, matrix products, dot_tn(): lax.dot_general(left, right, (((0,), (0,)), ((), ())), preferred_element_...  14.2 us
    dot_general x9, matrix products, dot_nt(): lax.dot_general(left, right, (((1,), (1,)), ((), ())), preferred_element_...  13 us
  transfers between devices with their start and end apart: 53, of which 19 were waited for; matrix products, arithmetic and copies ran while one was open for 32% of the time, Pallas kernels for 11%

profile of v2, /device:TPU:0, one launch (start us, length us, event | category | flops | bytes accessed | tf_op | source)
XLA Modules:
  0.0 465.1 jit_solution(7219848097636438155)
XLA Ops:
  3.0 4.0 collective-permute-start
  21.9 3.4 collective-permute-start.3
  29.2 2.1 select_select_fusion.low_ref
  36.0 8.9 %collective-permute-done.2 = bf16[2,2,96,576]{3,2,0,1:T(8,128)(2,1)S(1)} collective-permute-done((bf16[2,2,96,576]{3,2,0,1:T(8,128)(2,1)S(1)}, bf16[2,2,96,576]{3,2,0,1:T(8,128)(2,1)S(1)}, u32[]{:S(2)}, u32[]{:S(2)}) %collective-permute-start.2) | collective-permute-done | bytes 442400 | tf_op jit(solution)/shard_map/ppermute | solution.py:35
  47.6 3.0 multiply_convert_fusion.3.qkv_ref
  54.1 6.2 %shard_map.340 = (bf16[1024,192]{1,0:T(8,128)(2,1)S(1)}, f32[1024,192]{1,0:T(8,128)S(1)}) custom-call(s32[1024,1]{1,0:T(8,128)S(1)} %select_select_fusion.low_ref, bf16[1024,576]{1,0:T(8,128)(2,1)S(1)} %multiply_convert_fusion.3.qkv_ref), custom_call_target="tpu_custom_call" | custom-call | tf_op jit(solution)/shard_map/pallas_call | solution.py:208
  60.2 5.5 %collective-permute-done.7 = bf16[768,576]{0,1:T(8,128)(2,1)S(1)} collective-permute-done((bf16[768,576]{0,1:T(8,128)(2,1)S(1)}, bf16[768,576]{0,1:T(8,128)(2,1)S(1)}, u32[]{:S(2)}, u32[]{:S(2)}) %collective-permute-start.7) | collective-permute-done | bytes 884768 | tf_op jit(solution)/shard_map/ppermute | solution.py:35
  65.7 3.7 collective-permute-done.6
  74.6 6.5 %shard_map.341 = (bf16[1024,192]{1,0:T(8,128)(2,1)S(1)}, f32[1024,192]{1,0:T(8,128)S(1)}) custom-call(s32[1024,1]{1,0:T(8,128)S(1)} %select_select_fusion.low_ref, bf16[1024,576]{1,0:T(8,128)(2,1)S(1)} %multiply_convert_fusion.2.qkv_ref), custom_call_target="tpu_custom_call" | custom-call | tf_op jit(solution)/shard_map/pallas_call | solution.py:208
  81.1 22.9 %collective-permute-done.8 = bf16[768,192]{1,0:T(8,128)(2,1)S(1)} collective-permute-done((bf16[768,192]{1,0:T(8,128)(2,1)S(1)}, bf16[768,192]{1,0:T(8,128)(2,1)S(1)}, u32[]{:S(2)}, u32[]{:S(2)}) %collective-permute-start.8) | collective-permute-done | bytes 294944 | tf_op jit(solution)/shard_map/ppermute | solution.py:35
  114.8 14.6 %collective-permute-done.15 = bf16[2,2,2,96,768]{4,3,2,1,0:T(8,128)(2,1)} collective-permute-done((bf16[2,2,2,96,768]{4,3,2,1,0:T(8,128)(2,1)}, bf16[2,2,2,96,768]{4,3,2,1,0:T(8,128)(2,1)}, u32[]{:S(2)}, u32[]{:S(2)}) %collective-permute-start.15) | collective-permute-done | bytes 1179680 | tf_op jit(solution)/shard_map/ppermute | solution.py:35
  133.2 2.2 fusion.86
  141.5 3.5 convert_reduce_fusion.3
  145.0 3.7 convert_reduce_fusion.2
  166.2 3.6 convolution_convert_fusion
  169.8 2.5 convolution_convert_fusion.1
  172.3 2.3 multiply_reduce_fusion
  175.2 2.9 fusion.85
  183.1 10.6 %shard_map.342 = bf16[1024,576]{1,0:T(8,128)(2,1)S(1)} custom-call(s32[1024,1]{1,0:T(8,128)S(1)} %select_select_fusion.low_ref, bf16[1024,576]{1,0:T(8,128)(2,1)} %copy-done.1, bf16[1024,192]{1,0:T(8,128)(2,1)S(1)} %convolution_convert_fusion.7.grad_ref, f32[1024,192]{1,0:T(8,128)S(1)} %copy-done.3), custom_call_target="tpu_custom_call" | custom-call | tf_op jit(solution)/shard_map/pallas_call | solution.py:208
  195.4 3.5 add_add_fusion.3
  203.8 12.3 %collective-permute-done.20 = bf16[768,960]{0,1:T(8,128)(2,1)S(1)} collective-permute-done((bf16[768,960]{0,1:T(8,128)(2,1)S(1)}, bf16[768,960]{0,1:T(8,128)(2,1)S(1)}, u32[]{:S(2)}, u32[]{:S(2)}) %collective-permute-start.20) | collective-permute-done | bytes 1474592 | tf_op jit(solution)/shard_map/ppermute | solution.py:35
  218.1 3.5 copy.106
  221.6 2.2 fusion.34
  224.6 2.4 convolution_convert_fusion.5
  228.1 10.6 %shard_map.343 = bf16[1024,576]{1,0:T(8,128)(2,1)S(1)} custom-call(s32[1024,1]{1,0:T(8,128)S(1)} %select_select_fusion.low_ref, bf16[1024,576]{1,0:T(8,128)(2,1)} %copy-done, bf16[1024,192]{1,0:T(8,128)(2,1)S(1)} %convolution_convert_fusion.6.grad_ref, f32[1024,192]{1,0:T(8,128)S(1)} %get-tuple-element.179.log_ref), custom_call_target="tpu_custom_call" | custom-call | tf_op jit(solution)/shard_map/pallas_call | solution.py:208
  238.7 3.8 collective-permute-done.21
  256.4 2.6 convert_add_fusion.6
  265.0 2.4 collective-permute-start.27
  267.4 6.8 %collective-permute-done.29 = bf16[4,96,576]{2,1,0:T(8,128)(2,1)S(1)} collective-permute-done((bf16[4,96,576]{2,1,0:T(8,128)(2,1)S(1)}, bf16[4,96,576]{2,1,0:T(8,128)(2,1)S(1)}, u32[]{:S(2)}, u32[]{:S(2)}) %collective-permute-start.29) | collective-permute-done | bytes 442400 | tf_op jit(solution)/shard_map/ppermute | solution.py:35
  278.8 4.4 all-to-all-start
  289.9 4.4 fusion.24
  301.8 6.8 %collective-permute-done.30 = bf16[2,96,576]{2,1,0:T(8,128)(2,1)} collective-permute-done((bf16[2,96,576]{2,1,0:T(8,128)(2,1)}, bf16[2,96,576]{2,1,0:T(8,128)(2,1)}, u32[]{:S(2)}, u32[]{:S(2)}) %collective-permute-start.30) | collective-permute-done | bytes 221216 | tf_op jit(solution)/shard_map/ppermute | solution.py:35
  311.4 4.0 collective-permute-start.33
  315.4 2.7 fusion.102
  325.8 4.6 all-to-all-start.1
  334.8 7.4 %all-to-all-done.1 = bf16[8,96,192]{2,1,0:T(8,128)(2,1)S(1)} async-done(((bf16[8,96,192]{2,1,0:T(8,128)(2,1)}), bf16[8,96,192]{2,1,0:T(8,128)(2,1)S(1)}, u32[]{:S(2)}, u32[]{:S(2)}) %all-to-all-start.1) | async-done | bytes 294944 | tf_op jit(solution)/shard_map/all_to_all | solution.py:569
  345.7 3.8 fusion.83
  349.5 4.7 %collective-permute-done.36 = bf16[768,192]{1,0:T(8,128)(2,1)S(1)} collective-permute-done((bf16[768,192]{1,0:T(8,128)(2,1)S(1)}, bf16[768,192]{1,0:T(8,128)(2,1)S(1)}, u32[]{:S(2)}, u32[]{:S(2)}) %collective-permute-start.36) | collective-permute-done | bytes 294944 | tf_op jit(solution)/shard_map/ppermute | solution.py:35
  356.8 10.1 %collective-permute-done.34 = f32[192,768]{1,0:T(8,128)S(1)} collective-permute-done((f32[192,768]{1,0:T(8,128)}, f32[192,768]{1,0:T(8,128)S(1)}, u32[]{:S(2)}, u32[]{:S(2)}) %collective-permute-start.34) | collective-permute-done | bytes 589856 | tf_op jit(solution)/shard_map/ppermute | solution.py:35
  366.9 8.9 %collective-permute-done.35 = f32[192,768]{1,0:T(8,128)S(1)} collective-permute-done((f32[192,768]{1,0:T(8,128)}, f32[192,768]{1,0:T(8,128)S(1)}, u32[]{:S(2)}, u32[]{:S(2)}) %collective-permute-start.35) | collective-permute-done | bytes 589856 | tf_op jit(solution)/shard_map/ppermute | solution.py:35
  381.7 3.0 collective-permute-start.44
  391.0 2.2 pad_maximum_fusion.2
  394.6 18.4 %shard_map.344 = bf16[768,768]{1,0:T(8,128)(2,1)} custom-call(s32[1]{0:T(128)} %bitcast.86.wide_ref, f32[1]{0:T(128)} %bitcast.89.factor_ref, f32[20]{0:T(128)S(1)} %copy-done.6, f32[768,768]{1,0:T(8,128)} %bitcast.393, bf16[768,768]{1,0:T(8,128)(2,1)S(1)} %get-tuple-element.280.panel_ref), custom_call_target="tpu_custom_call" | custom-call | flops 22649241600 | bytes 5242880 | tf_op jit(solution)/shard_map/pallas_call | solution.py:340
  413.0 10.5 %collective-permute-done.42 = bf16[512,768]{1,0:T(8,128)(2,1)} collective-permute-done((bf16[512,768]{1,0:T(8,128)(2,1)S(1)}, bf16[512,768]{1,0:T(8,128)(2,1)}, u32[]{:S(2)}, u32[]{:S(2)}) %collective-permute-start.42) | collective-permute-done | bytes 786464 | tf_op jit(solution)/shard_map/ppermute | solution.py:35
  425.6 7.8 %all-to-all-start.2 = ((bf16[8,96,768]{2,1,0:T(8,128)(2,1)}), bf16[8,96,768]{2,1,0:T(8,128)(2,1)S(1)}, u32[]{:S(2)}, u32[]{:S(2)}) async-start(bf16[8,96,768]{2,1,0:T(8,128)(2,1)} %bitcast.106), calls=%async_computation.2 | async-start | bytes 2359296 | tf_op jit(solution)/shard_map/all_to_all | solution.py:610
  447.9 3.4 bitcast_convert_fusion
  451.2 3.4 bitcast_convert_fusion.1
  454.6 6.8 %all-to-all-done.2 = bf16[8,96,768]{2,1,0:T(8,128)(2,1)S(1)} async-done(((bf16[8,96,768]{2,1,0:T(8,128)(2,1)}), bf16[8,96,768]{2,1,0:T(8,128)(2,1)S(1)}, u32[]{:S(2)}, u32[]{:S(2)}) %all-to-all-start.2) | async-done | bytes 1179680 | tf_op jit(solution)/shard_map/all_to_all | solution.py:610
  (486 shorter events, 181.3 us)
Async XLA Ops:
  3.0 10.3 %collective-permute-start = (bf16[96,576]{1,0:T(8,128)(2,1)}, bf16[96,576]{1,0:T(8,128)(2,1)}, u32[]{:S(2)}, u32[]{:S(2)}) collective-permute-start(bf16[96,576]{1,0:T(8,128)(2,1)} %pad_maximum_fusion.25), channel_id=1, source_target_pairs={{0,16},{8,24},{16,0},{24,8},{1,17},{9,25},{17,1},{25,9},{2,18},{10... | collective-permute-start | bytes 331784 | tf_op jit(solution)/shard_map/ppermute | solution.py:35
  16.6 14.8 %collective-permute-start.10 = (f32[1152]{0:T(1024)}, f32[1152]{0:T(1024)S(1)}, u32[]{:S(2)}, u32[]{:S(2)}) collective-permute-start(f32[1152]{0:T(1024)} %pad_maximum_fusion.27), channel_id=1, source_target_pairs={{0,2},{2,0},{1,3},{3,1},{4,6},{6,4},{5,7},{7,5},{8,10},{10,8},{9,1... | collective-permute-start | bytes 13832 | tf_op jit(solution)/shard_map/ppermute | solution.py:35
  18.1 13.4 %collective-permute-start.1 = (bf16[2,96,576]{2,1,0:T(8,128)(2,1)}, bf16[2,96,576]{2,1,0:T(8,128)(2,1)}, u32[]{:S(2)}, u32[]{:S(2)}) collective-permute-start(bf16[2,96,576]{2,1,0:T(8,128)(2,1)} %pad_maximum_fusion.23), channel_id=1, source_target_pairs={{0,8},{8,0},{16,24},{24,16},{1,9},{9,1},{17,25},{25,17},{2,10},{10... | collective-permute-start | bytes 663560 | tf_op jit(solution)/shard_map/ppermute | solution.py:35
  21.3 13.1 %collective-permute-start.4 = (bf16[96,768]{1,0:T(8,128)(2,1)S(1)}, bf16[96,768]{1,0:T(8,128)(2,1)S(1)}, u32[]{:S(2)}, u32[]{:S(2)}) collective-permute-start(bf16[96,768]{1,0:T(8,128)(2,1)S(1)} %bitcast.394), channel_id=1, source_target_pairs={{0,2},{2,0},{1,3},{3,1},{4,6},{6,4},{5,7},{7,5},{8,10},{10,8},{9,1... | collective-permute-start | bytes 442376 | tf_op jit(solution)/shard_map/ppermute | solution.py:35
  21.9 12.4 %collective-permute-start.3 = (bf16[96,960]{1,0:T(8,128)(2,1)S(1)}, bf16[96,960]{1,0:T(8,128)(2,1)S(1)}, u32[]{:S(2)}, u32[]{:S(2)}) collective-permute-start(bf16[96,960]{1,0:T(8,128)(2,1)S(1)} %pad_maximum_fusion.24), channel_id=1, source_target_pairs={{0,16},{8,24},{16,0},{24,8},{1,17},{9,25},{17,1},{25,9},{2,18},{10... | collective-permute-start | bytes 552968 | tf_op jit(solution)/shard_map/ppermute | solution.py:35
  32.7 12.1 %collective-permute-start.2 = (bf16[2,2,96,576]{3,2,0,1:T(8,128)(2,1)S(1)}, bf16[2,2,96,576]{3,2,0,1:T(8,128)(2,1)S(1)}, u32[]{:S(2)}, u32[]{:S(2)}) collective-permute-start(bf16[2,2,96,576]{3,2,0,1:T(8,128)(2,1)S(1)} %pad_maximum_fusion.19), channel_id=1, source_target_pairs={{0,4},{4,0},{1,5},{5,1},{2,6},{6,2},{3,7},{7,3},{8,12},{12,8},{9,1... | collective-permute-start | bytes 1327112 | tf_op jit(solution)/shard_map/ppermute | solution.py:35
  35.2 15.4 %collective-permute-start.5 = (bf16[2,96,960]{2,1,0:T(8,128)(2,1)}, bf16[2,96,960]{2,1,0:T(8,128)(2,1)}, u32[]{:S(2)}, u32[]{:S(2)}) collective-permute-start(bf16[2,96,960]{2,1,0:T(8,128)(2,1)} %pad_maximum_fusion.20), channel_id=1, source_target_pairs={{0,8},{8,0},{16,24},{24,16},{1,9},{9,1},{17,25},{25,17},{2,10},{10... | collective-permute-start | bytes 1105928 | tf_op jit(solution)/shard_map/ppermute | solution.py:35
  46.0 19.7 %collective-permute-start.7 = (bf16[768,576]{0,1:T(8,128)(2,1)S(1)}, bf16[768,576]{0,1:T(8,128)(2,1)S(1)}, u32[]{:S(2)}, u32[]{:S(2)}) collective-permute-start(bf16[768,576]{0,1:T(8,128)(2,1)S(1)} %copy.97), channel_id=1, source_target_pairs={{0,2},{2,0},{1,3},{3,1},{4,6},{6,4},{5,7},{7,5},{8,10},{10,8},{9,1... | collective-permute-start | bytes 2654216 | tf_op jit(solution)/shard_map/ppermute | solution.py:35
  52.2 17.3 %collective-permute-start.6 = (bf16[2,2,96,960]{3,2,0,1:T(8,128)(2,1)S(1)}, bf16[2,2,96,960]{3,2,0,1:T(8,128)(2,1)S(1)}, u32[]{:S(2)}, u32[]{:S(2)}) collective-permute-start(bf16[2,2,96,960]{3,2,0,1:T(8,128)(2,1)S(1)} %pad_maximum_fusion.16), channel_id=1, source_target_pairs={{0,4},{4,0},{1,5},{5,1},{2,6},{6,2},{3,7},{7,3},{8,12},{12,8},{9,1... | collective-permute-start | bytes 2211848 | tf_op jit(solution)/shard_map/ppermute | solution.py:35
  53.8 16.3 %collective-permute-start.9 = (bf16[2,96,768]{2,1,0:T(8,128)(2,1)S(1)}, bf16[2,96,768]{2,1,0:T(8,128)(2,1)S(1)}, u32[]{:S(2)}, u32[]{:S(2)}) collective-permute-start(bf16[2,96,768]{2,1,0:T(8,128)(2,1)S(1)} %copy-done.74), channel_id=1, source_target_pairs={{0,16},{8,24},{16,0},{24,8},{1,17},{9,25},{17,1},{25,9},{2,18},{10... | collective-permute-start | bytes 884744 | tf_op jit(solution)/shard_map/ppermute | solution.py:35
  70.2 33.8 %collective-permute-start.12 = (bf16[2,2,96,768]{3,2,1,0:T(8,128)(2,1)S(1)}, bf16[2,2,96,768]{3,2,1,0:T(8,128)(2,1)S(1)}, u32[]{:S(2)}, u32[]{:S(2)}) collective-permute-start(bf16[2,2,96,768]{3,2,1,0:T(8,128)(2,1)S(1)} %pad_maximum_fusion.17), channel_id=1, source_target_pairs={{0,8},{8,0},{16,24},{24,16},{1,9},{9,1},{17,25},{25,17},{2,10},{10... | collective-permute-start | bytes 1769480 | tf_op jit(solution)/shard_map/ppermute | solution.py:35
  70.8 36.6 %collective-permute-start.11 = (bf16[768,768]{1,0:T(8,128)(2,1)S(1)}, bf16[768,768]{1,0:T(8,128)(2,1)S(1)}, u32[]{:S(2)}, u32[]{:S(2)}) collective-permute-start(bf16[768,768]{1,0:T(8,128)(2,1)S(1)} %slice.454), channel_id=1, source_target_pairs={{0,2},{2,0},{1,3},{3,1},{4,6},{6,4},{5,7},{7,5},{8,10},{10,8},{9,1... | collective-permute-start | bytes 3538952 | tf_op jit(solution)/shard_map/ppermute | solution.py:35
  71.4 32.6 %collective-permute-start.8 = (bf16[768,192]{1,0:T(8,128)(2,1)S(1)}, bf16[768,192]{1,0:T(8,128)(2,1)S(1)}, u32[]{:S(2)}, u32[]{:S(2)}) collective-permute-start(bf16[768,192]{1,0:T(8,128)(2,1)S(1)} %slice.453), channel_id=1, source_target_pairs={{0,2},{2,0},{1,3},{3,1},{4,6},{6,4},{5,7},{7,5},{8,10},{10,8},{9,1... | collective-permute-start | bytes 884744 | tf_op jit(solution)/shard_map/ppermute | solution.py:35
  105.2 24.2 %collective-permute-start.15 = (bf16[2,2,2,96,768]{4,3,2,1,0:T(8,128)(2,1)}, bf16[2,2,2,96,768]{4,3,2,1,0:T(8,128)(2,1)}, u32[]{:S(2)}, u32[]{:S(2)}) collective-permute-start(bf16[2,2,2,96,768]{4,3,2,1,0:T(8,128)(2,1)} %pad_maximum_fusion.11), channel_id=1, source_target_pairs={{0,4},{4,0},{1,5},{5,1},{2,6},{6,2},{3,7},{7,3},{8,12},{12,8},{9,1... | collective-permute-start | bytes 3538952 | tf_op jit(solution)/shard_map/ppermute | solution.py:35
  110.8 20.2 %collective-permute-start.13 = (bf16[512,768]{1,0:T(8,128)(2,1)}, bf16[512,768]{1,0:T(8,128)(2,1)}, u32[]{:S(2)}, u32[]{:S(2)}) collective-permute-start(bf16[512,768]{1,0:T(8,128)(2,1)} %get-tuple-element.321), channel_id=1, source_target_pairs={{0,1},{1,0},{2,3},{3,2},{4,5},{5,4},{6,7},{7,6},{8,9},{9,8},{10,11... | collective-permute-start | bytes 2359304 | tf_op jit(solution)/shard_map/ppermute | solution.py:35
  110.8 20.3 %collective-permute-start.14 = (bf16[512,768]{1,0:T(8,128)(2,1)}, bf16[512,768]{1,0:T(8,128)(2,1)}, u32[]{:S(2)}, u32[]{:S(2)}) collective-permute-start(bf16[512,768]{1,0:T(8,128)(2,1)} %get-tuple-element.322), channel_id=1, source_target_pairs={{0,1},{1,0},{2,3},{3,2},{4,5},{5,4},{6,7},{7,6},{8,9},{9,8},{10,11... | collective-permute-start | bytes 2359304 | tf_op jit(solution)/shard_map/ppermute | solution.py:35
  159.2 39.7 %collective-permute-start.22 = (bf16[2,4,96,768]{3,2,1,0:T(8,128)(2,1)}, bf16[2,4,96,768]{3,2,1,0:T(8,128)(2,1)}, u32[]{:S(2)}, u32[]{:S(2)}) collective-permute-start(bf16[2,4,96,768]{3,2,1,0:T(8,128)(2,1)} %select_bitcast_fusion.2), channel_id=1, source_target_pairs={{0,4},{4,0},{1,5},{5,1},{2,6},{6,2},{3,7},{7,3},{8,12},{12,8},{9,1... | collective-permute-start | bytes 3538952 | tf_op jit(solution)/shard_map/ppermute | solution.py:35
  160.7 11.6 %collective-permute-start.18 = (bf16[512,768]{1,0:T(8,128)(2,1)}, bf16[512,768]{1,0:T(8,128)(2,1)S(1)}, u32[]{:S(2)}, u32[]{:S(2)}) collective-permute-start(bf16[512,768]{1,0:T(8,128)(2,1)} %get-tuple-element.317), channel_id=1, source_target_pairs={{0,1},{1,0},{2,3},{3,2},{4,5},{5,4},{6,7},{7,6},{8,9},{9,8},{10,11... | collective-permute-start | bytes 2359304 | tf_op jit(solution)/shard_map/ppermute | solution.py:35
  160.7 11.6 %collective-permute-start.19 = (bf16[512,768]{1,0:T(8,128)(2,1)}, bf16[512,768]{1,0:T(8,128)(2,1)}, u32[]{:S(2)}, u32[]{:S(2)}) collective-permute-start(bf16[512,768]{1,0:T(8,128)(2,1)} %get-tuple-element.318), channel_id=1, source_target_pairs={{0,1},{1,0},{2,3},{3,2},{4,5},{5,4},{6,7},{7,6},{8,9},{9,8},{10,11... | collective-permute-start | bytes 2359304 | tf_op jit(solution)/shard_map/ppermute | solution.py:35
  165.7 29.6 %collective-permute-start.16 = (bf16[512,768]{1,0:T(8,128)(2,1)}, bf16[512,768]{1,0:T(8,128)(2,1)}, u32[]{:S(2)}, u32[]{:S(2)}) collective-permute-start(bf16[512,768]{1,0:T(8,128)(2,1)} %get-tuple-element.319), channel_id=1, source_target_pairs={{0,1},{1,0},{2,3},{3,2},{4,5},{5,4},{6,7},{7,6},{8,9},{9,8},{10,11... | collective-permute-start | bytes 2359304 | tf_op jit(solution)/shard_map/ppermute | solution.py:35
  165.7 29.6 %collective-permute-start.17 = (bf16[512,768]{1,0:T(8,128)(2,1)}, bf16[512,768]{1,0:T(8,128)(2,1)}, u32[]{:S(2)}, u32[]{:S(2)}) collective-permute-start(bf16[512,768]{1,0:T(8,128)(2,1)} %get-tuple-element.320), channel_id=1, source_target_pairs={{0,1},{1,0},{2,3},{3,2},{4,5},{5,4},{6,7},{7,6},{8,9},{9,8},{10,11... | collective-permute-start | bytes 2359304 | tf_op jit(solution)/shard_map/ppermute | solution.py:35
  182.0 34.1 %collective-permute-start.20 = (bf16[768,960]{0,1:T(8,128)(2,1)S(1)}, bf16[768,960]{0,1:T(8,128)(2,1)S(1)}, u32[]{:S(2)}, u32[]{:S(2)}) collective-permute-start(bf16[768,960]{0,1:T(8,128)(2,1)S(1)} %pad_maximum_fusion.8), channel_id=1, source_target_pairs={{0,2},{2,0},{1,3},{3,1},{4,6},{6,4},{5,7},{7,5},{8,10},{10,8},{9,1... | collective-permute-start | bytes 4423688 | tf_op jit(solution)/shard_map/ppermute | solution.py:35
  202.9 42.2 %collective-permute-start.24 = (bf16[2,2,96,768]{3,2,1,0:T(8,128)(2,1)}, bf16[2,2,96,768]{3,2,1,0:T(8,128)(2,1)}, u32[]{:S(2)}, u32[]{:S(2)}) collective-permute-start(bf16[2,2,96,768]{3,2,1,0:T(8,128)(2,1)} %fusion.35), channel_id=1, source_target_pairs={{0,8},{8,0},{16,24},{24,16},{1,9},{9,1},{17,25},{25,17},{2,10},{10... | collective-permute-start | bytes 1769480 | tf_op jit(solution)/shard_map/ppermute | solution.py:35
  223.7 18.8 %collective-permute-start.21 = (bf16[4,96,960]{2,1,0:T(8,128)(2,1)S(1)}, bf16[4,96,960]{2,1,0:T(8,128)(2,1)}, u32[]{:S(2)}, u32[]{:S(2)}) collective-permute-start(bf16[4,96,960]{2,1,0:T(8,128)(2,1)S(1)} %fusion.34), channel_id=1, source_target_pairs={{0,4},{4,0},{1,5},{5,1},{2,6},{6,2},{3,7},{7,3},{8,12},{12,8},{9,1... | collective-permute-start | bytes 2211848 | tf_op jit(solution)/shard_map/ppermute | solution.py:35
  227.6 28.8 %collective-permute-start.26 = (bf16[768,576]{0,1:T(8,128)(2,1)}, bf16[768,576]{0,1:T(8,128)(2,1)}, u32[]{:S(2)}, u32[]{:S(2)}) collective-permute-start(bf16[768,576]{0,1:T(8,128)(2,1)} %convolution_convert_fusion.5), channel_id=1, source_target_pairs={{0,2},{2,0},{1,3},{3,1},{4,6},{6,4},{5,7},{7,5},{8,10},{10,8},{9,1... | collective-permute-start | bytes 2654216 | tf_op jit(solution)/shard_map/ppermute | solution.py:35
  247.3 14.8 %collective-permute-start.25 = (bf16[2,96,768]{2,1,0:T(8,128)(2,1)}, bf16[2,96,768]{2,1,0:T(8,128)(2,1)}, u32[]{:S(2)}, u32[]{:S(2)}) collective-permute-start(bf16[2,96,768]{2,1,0:T(8,128)(2,1)} %fusion.42), channel_id=1, source_target_pairs={{0,16},{8,24},{16,0},{24,8},{1,17},{9,25},{17,1},{25,9},{2,18},{10... | collective-permute-start | bytes 884744 | tf_op jit(solution)/shard_map/ppermute | solution.py:35
  248.0 15.8 %collective-permute-start.23 = (bf16[2,96,960]{2,1,0:T(8,128)(2,1)}, bf16[2,96,960]{2,1,0:T(8,128)(2,1)}, u32[]{:S(2)}, u32[]{:S(2)}) collective-permute-start(bf16[2,96,960]{2,1,0:T(8,128)(2,1)} %fusion.41), channel_id=1, source_target_pairs={{0,8},{8,0},{16,24},{24,16},{1,9},{9,1},{17,25},{25,17},{2,10},{10... | collective-permute-start | bytes 1105928 | tf_op jit(solution)/shard_map/ppermute | solution.py:35
  254.1 35.8 %collective-permute-start.38 = (bf16[512,768]{1,0:T(8,128)(2,1)}, bf16[512,768]{1,0:T(8,128)(2,1)}, u32[]{:S(2)}, u32[]{:S(2)}) collective-permute-start(bf16[512,768]{1,0:T(8,128)(2,1)} %get-tuple-element.315), channel_id=1, source_target_pairs={{0,1},{1,0},{2,3},{3,2},{4,5},{5,4},{6,7},{7,6},{8,9},{9,8},{10,11... | collective-permute-start | bytes 2359304 | tf_op jit(solution)/shard_map/ppermute | solution.py:35
  254.1 35.8 %collective-permute-start.39 = (bf16[512,768]{1,0:T(8,128)(2,1)}, bf16[512,768]{1,0:T(8,128)(2,1)}, u32[]{:S(2)}, u32[]{:S(2)}) collective-permute-start(bf16[512,768]{1,0:T(8,128)(2,1)} %get-tuple-element.316), channel_id=1, source_target_pairs={{0,1},{1,0},{2,3},{3,2},{4,5},{5,4},{6,7},{7,6},{8,9},{9,8},{10,11... | collective-permute-start | bytes 2359304 | tf_op jit(solution)/shard_map/ppermute | solution.py:35
  261.1 13.2 %collective-permute-start.29 = (bf16[4,96,576]{2,1,0:T(8,128)(2,1)S(1)}, bf16[4,96,576]{2,1,0:T(8,128)(2,1)S(1)}, u32[]{:S(2)}, u32[]{:S(2)}) collective-permute-start(bf16[4,96,576]{2,1,0:T(8,128)(2,1)S(1)} %fusion.40), channel_id=1, source_target_pairs={{0,4},{4,0},{1,5},{5,1},{2,6},{6,2},{3,7},{7,3},{8,12},{12,8},{9,1... | collective-permute-start | bytes 1327112 | tf_op jit(solution)/shard_map/ppermute | solution.py:35
  263.2 12.1 %collective-permute-start.28 = (bf16[96,768]{1,0:T(8,128)(2,1)S(1)}, bf16[96,768]{1,0:T(8,128)(2,1)S(1)}, u32[]{:S(2)}, u32[]{:S(2)}) collective-permute-start(bf16[96,768]{1,0:T(8,128)(2,1)S(1)} %fusion.52), channel_id=1, source_target_pairs={{0,2},{2,0},{1,3},{3,1},{4,6},{6,4},{5,7},{7,5},{8,10},{10,8},{9,1... | collective-permute-start | bytes 442376 | tf_op jit(solution)/shard_map/ppermute | solution.py:35
  265.0 11.1 %collective-permute-start.27 = (bf16[96,960]{1,0:T(8,128)(2,1)S(1)}, bf16[96,960]{1,0:T(8,128)(2,1)S(1)}, u32[]{:S(2)}, u32[]{:S(2)}) collective-permute-start(bf16[96,960]{1,0:T(8,128)(2,1)S(1)} %fusion.48), channel_id=1, source_target_pairs={{0,16},{8,24},{16,0},{24,8},{1,17},{9,25},{17,1},{25,9},{2,18},{10... | collective-permute-start | bytes 552968 | tf_op jit(solution)/shard_map/ppermute | solution.py:35
  278.8 36.6 %all-to-all-start = ((bf16[8,96,768]{2,1,0:T(8,128)(2,1)}), bf16[8,96,768]{2,1,0:T(8,128)(2,1)}, u32[]{:S(2)}, u32[]{:S(2)}) async-start(bf16[8,96,768]{2,1,0:T(8,128)(2,1)} %copy-done.38), calls=%async_computation | async-start | bytes 2359296 | tf_op jit(solution)/shard_map/all_to_all | solution.py:569
  284.7 23.9 %collective-permute-start.30 = (bf16[2,96,576]{2,1,0:T(8,128)(2,1)}, bf16[2,96,576]{2,1,0:T(8,128)(2,1)}, u32[]{:S(2)}, u32[]{:S(2)}) collective-permute-start(bf16[2,96,576]{2,1,0:T(8,128)(2,1)} %fusion.47), channel_id=1, source_target_pairs={{0,8},{8,0},{16,24},{24,16},{1,9},{9,1},{17,25},{25,17},{2,10},{10... | collective-permute-start | bytes 663560 | tf_op jit(solution)/shard_map/ppermute | solution.py:35
  299.0 55.6 %collective-permute-start.40 = (f32[54,128]{1,0:T(8,128)}, f32[54,128]{1,0:T(8,128)}, u32[]{:S(2)}, u32[]{:S(2)}) collective-permute-start(f32[54,128]{1,0:T(8,128)} %maximum_bitcast_fusion), channel_id=1, source_target_pairs={{0,2},{2,0},{1,3},{3,1},{4,6},{6,4},{5,7},{7,5},{8,10},{10,8},{9,1... | collective-permute-start | bytes 82952 | tf_op jit(solution)/shard_map/ppermute | solution.py:35
  311.4 9.4 %collective-permute-start.33 = (bf16[96,576]{1,0:T(8,128)(2,1)}, bf16[96,576]{1,0:T(8,128)(2,1)}, u32[]{:S(2)}, u32[]{:S(2)}) collective-permute-start(bf16[96,576]{1,0:T(8,128)(2,1)} %fusion.53), channel_id=1, source_target_pairs={{0,16},{8,24},{16,0},{24,8},{1,17},{9,25},{17,1},{25,9},{2,18},{10... | collective-permute-start | bytes 331784 | tf_op jit(solution)/shard_map/ppermute | solution.py:35
  325.8 16.4 %all-to-all-start.1 = ((bf16[8,96,192]{2,1,0:T(8,128)(2,1)}), bf16[8,96,192]{2,1,0:T(8,128)(2,1)S(1)}, u32[]{:S(2)}, u32[]{:S(2)}) async-start(bf16[8,96,192]{2,1,0:T(8,128)(2,1)} %fusion.61), calls=%async_computation.1 | async-start | bytes 786432 | tf_op jit(solution)/shard_map/all_to_all | solution.py:569
  342.2 12.1 %collective-permute-start.36 = (bf16[768,192]{1,0:T(8,128)(2,1)S(1)}, bf16[768,192]{1,0:T(8,128)(2,1)S(1)}, u32[]{:S(2)}, u32[]{:S(2)}) collective-permute-start(bf16[768,192]{1,0:T(8,128)(2,1)S(1)} %bitcast.390), channel_id=1, source_target_pairs={{0,2},{2,0},{1,3},{3,1},{4,6},{6,4},{5,7},{7,5},{8,10},{10,8},{9,1... | collective-permute-start | bytes 884744 | tf_op jit(solution)/shard_map/ppermute | solution.py:35
  343.7 23.2 %collective-permute-start.34 = (f32[192,768]{1,0:T(8,128)}, f32[192,768]{1,0:T(8,128)S(1)}, u32[]{:S(2)}, u32[]{:S(2)}) collective-permute-start(f32[192,768]{1,0:T(8,128)} %get-tuple-element.327), channel_id=1, source_target_pairs={{0,2},{2,0},{1,3},{3,1},{4,6},{6,4},{5,7},{7,5},{8,10},{10,8},{9,1... | collective-permute-start | bytes 1769480 | tf_op jit(solution)/shard_map/ppermute | solution.py:35
  344.2 31.6 %collective-permute-start.35 = (f32[192,768]{1,0:T(8,128)}, f32[192,768]{1,0:T(8,128)S(1)}, u32[]{:S(2)}, u32[]{:S(2)}) collective-permute-start(f32[192,768]{1,0:T(8,128)} %get-tuple-element.328), channel_id=1, source_target_pairs={{0,2},{2,0},{1,3},{3,1},{4,6},{6,4},{5,7},{7,5},{8,10},{10,8},{9,1... | collective-permute-start | bytes 1769480 | tf_op jit(solution)/shard_map/ppermute | solution.py:35
  354.5 21.4 %collective-permute-start.37 = (bf16[768,384]{1,0:T(8,128)(2,1)S(1)}, bf16[768,384]{1,0:T(8,128)(2,1)S(1)}, u32[]{:S(2)}, u32[]{:S(2)}) collective-permute-start(bf16[768,384]{1,0:T(8,128)(2,1)S(1)} %pad_maximum_fusion.18), channel_id=1, source_target_pairs={{0,1},{1,0},{2,3},{3,2},{4,5},{5,4},{6,7},{7,6},{8,9},{9,8},{10,11... | collective-permute-start | bytes 1769480 | tf_op jit(solution)/shard_map/ppermute | solution.py:35
  355.4 21.1 %collective-permute-start.41 = (f32[54,128]{1,0:T(8,128)S(1)}, f32[54,128]{1,0:T(8,128)S(1)}, u32[]{:S(2)}, u32[]{:S(2)}) collective-permute-start(f32[54,128]{1,0:T(8,128)S(1)} %fusion.146), channel_id=1, source_target_pairs={{0,4},{4,0},{1,5},{5,1},{2,6},{6,2},{3,7},{7,3},{8,12},{12,8},{9,1... | collective-permute-start | bytes 82952 | tf_op jit(solution)/shard_map/ppermute | solution.py:35
  377.8 12.4 %collective-permute-start.46 = (f32[192,768]{1,0:T(8,128)S(1)}, f32[192,768]{1,0:T(8,128)S(1)}, u32[]{:S(2)}, u32[]{:S(2)}) collective-permute-start(f32[192,768]{1,0:T(8,128)S(1)} %get-tuple-element.326), channel_id=1, source_target_pairs={{0,1},{1,0},{2,3},{3,2},{4,5},{5,4},{6,7},{7,6},{8,9},{9,8},{10,11... | collective-permute-start | bytes 1769480 | tf_op jit(solution)/shard_map/ppermute | solution.py:35
  380.7 9.6 %collective-permute-start.47 = (f32[192,768]{1,0:T(8,128)S(1)}, f32[192,768]{1,0:T(8,128)S(1)}, u32[]{:S(2)}, u32[]{:S(2)}) collective-permute-start(f32[192,768]{1,0:T(8,128)S(1)} %get-tuple-element.325), channel_id=1, source_target_pairs={{0,1},{1,0},{2,3},{3,2},{4,5},{5,4},{6,7},{7,6},{8,9},{9,8},{10,11... | collective-permute-start | bytes 1769480 | tf_op jit(solution)/shard_map/ppermute | solution.py:35
  386.9 26.1 %collective-permute-start.43 = (bf16[512,768]{1,0:T(8,128)(2,1)}, bf16[512,768]{1,0:T(8,128)(2,1)}, u32[]{:S(2)}, u32[]{:S(2)}) collective-permute-start(bf16[512,768]{1,0:T(8,128)(2,1)} %constant_dynamic-slice_fusion.1), channel_id=1, source_target_pairs={{0,2},{2,0},{1,3},{3,1},{4,6},{6,4},{5,7},{7,5},{8,10},{10,8},{9,1... | collective-permute-start | bytes 2359304 | tf_op jit(solution)/shard_map/ppermute | solution.py:35
  388.4 35.2 %collective-permute-start.42 = (bf16[512,768]{1,0:T(8,128)(2,1)S(1)}, bf16[512,768]{1,0:T(8,128)(2,1)}, u32[]{:S(2)}, u32[]{:S(2)}) collective-permute-start(bf16[512,768]{1,0:T(8,128)(2,1)S(1)} %constant_dynamic-slice_fusion.2), channel_id=1, source_target_pairs={{0,2},{2,0},{1,3},{3,1},{4,6},{6,4},{5,7},{7,5},{8,10},{10,8},{9,1... | collective-permute-start | bytes 2359304 | tf_op jit(solution)/shard_map/ppermute | solution.py:35
  389.6 23.4 %collective-permute-start.45 = (f32[54,128]{1,0:T(8,128)}, f32[54,128]{1,0:T(8,128)}, u32[]{:S(2)}, u32[]{:S(2)}) collective-permute-start(f32[54,128]{1,0:T(8,128)} %add.439), channel_id=1, source_target_pairs={{0,8},{8,0},{16,24},{24,16},{1,9},{9,1},{17,25},{25,17},{2,10},{10... | collective-permute-start | bytes 82952 | tf_op jit(solution)/shard_map/ppermute | solution.py:35
  425.6 35.8 %all-to-all-start.2 = ((bf16[8,96,768]{2,1,0:T(8,128)(2,1)}), bf16[8,96,768]{2,1,0:T(8,128)(2,1)S(1)}, u32[]{:S(2)}, u32[]{:S(2)}) async-start(bf16[8,96,768]{2,1,0:T(8,128)(2,1)} %bitcast.106), calls=%async_computation.2 | async-start | bytes 2359296 | tf_op jit(solution)/shard_map/all_to_all | solution.py:610
  (113 other events, 1241.5 us)
